TPU v7x, 256 devices: a whole 4x4x8 slice. The times are simulated.
256 devices in a mesh: section: 8 (over x, core), ctx: 32 (over z, y).
Axes of the slice: x: 4, y: 4, z: 8, core: 2. Of those that a mesh axis runs over, the one named last changes fastest.
Arguments:
- section_input: bfloat16 [8, 4096, 8192], P('section', 'ctx'), may hold values from -6 to 6
- norm_gain: bfloat16 [8, 8192], P('section'), may hold values from 0.099609375 to 1.8984375
- conv_weight: bfloat16 [8, 4, 8192], P('section'), may hold values from -3 to 3
- state_write: bfloat16 [8, 4096, 1024], P('section', 'ctx'), may hold values from -6 to 6
- state_read: bfloat16 [8, 4096, 1024], P('section', 'ctx'), may hold values from -6 to 6
- step_size: float32 [8, 128, 4096], P('section', None, 'ctx'), as said below
- log_decay: float32 [8, 128, 4096], P('section', None, 'ctx'), may hold values from -1 to 0, as said below
- skip_gain: float32 [8, 128], P('section'), may hold values from 0.1 to 1.9
Outputs:
- handed: bfloat16 [8, 4096, 8192], P('section', 'ctx')
Inputs may be any that keep to these rules, and one draw needn't show every extreme that they name: `step_size`: positive. `log_decay`: never positive.
All inputs are finite; a program needn't handle non-finite values.
Results may differ from a plain program's by a relative error of at most 0.01.
Values may be sent and summed in bfloat16 or wider, within the bound.
A program may use at most 320 MiB of HBM per device.

v0:
```python
import jax
import jax.numpy as jnp
from jax import lax
from jax.sharding import PartitionSpec as P

HEADS = 128
HEAD_DIM = 64
STATE = 128
GROUPS = 8
CONV = 4
SPAN = 128


def passed_along(block, axis, distance):
    devices = range(lax.axis_size(axis))
    route = [(i - distance, i) for i in devices if i - distance in devices]
    return lax.ppermute(block, axis, route)


def entering_2(value, axis, combine, identity):
    count, position = (lax.axis_size(axis), lax.axis_index(axis))
    everything = jax.tree.map(lambda part: lax.all_gather(part, axis), value)
    start = jax.tree.map(
        lambda part, zero: jnp.broadcast_to(jnp.asarray(zero, part.dtype), part.shape),
        value,
        identity,
    )

    def step(k, before):
        reached = k < position
        new = combine(before, jax.tree.map(lambda part: part[k], everything))
        return jax.tree.map(lambda a, b: jnp.where(reached, a, b), new, before)

    return lax.fori_loop(0, count, step, start)


def from_behind(block, axis, distance):
    devices = range(lax.axis_size(axis))
    route = [((i - distance) % len(devices), i) for i in devices]
    return lax.ppermute(block, axis, route)


def block_parts(mixed, writes, reads, steps, decays):
    per_group = HEADS // GROUPS
    cumul = jnp.cumsum(decays, axis=-1)
    scores = jnp.einsum("tgn,sgn->gts", reads, writes, preferred_element_type=jnp.float32)
    scores = jnp.repeat(scores, per_group, axis=0)
    spread = cumul[:, :, None] - cumul[:, None, :]
    lower = jnp.arange(SPAN)[:, None] >= jnp.arange(SPAN)[None, :]
    weights = jnp.where(
        lower[None], scores * jnp.exp(jnp.minimum(spread, 0.0)) * steps[:, None, :], 0.0
    ).astype(jnp.bfloat16)
    inner = jnp.einsum("hts,shp->thp", weights, mixed, preferred_element_type=jnp.float32)
    to_end = jnp.exp(cumul[:, -1:] - cumul) * steps
    scaled = (mixed.astype(jnp.float32) * jnp.transpose(to_end)[:, :, None]).astype(jnp.bfloat16)
    scaled = scaled.reshape(SPAN, GROUPS, per_group, HEAD_DIM)
    summary = jnp.einsum("sgn,sgkp->gknp", writes, scaled, preferred_element_type=jnp.float32)
    summary = summary.reshape(HEADS, STATE, HEAD_DIM)
    return (inner, jnp.exp(cumul[:, -1]), summary, cumul)


def carried_term(reads, cumul, entering):
    grouped = entering.reshape(GROUPS, HEADS // GROUPS, STATE, HEAD_DIM)
    term = jnp.einsum("tgn,gknp->tgkp", reads, grouped, preferred_element_type=jnp.float32)
    term = term.reshape(SPAN, HEADS, HEAD_DIM)
    return term * jnp.transpose(jnp.exp(cumul))[:, :, None]


def combine(earlier, later):
    return (earlier[0] * later[0], later[0][:, None, None] * earlier[1] + later[1])


def layer_body(stream, gain, conv_taps, writes, reads, steps, decays, skip):
    rows, width = stream.shape
    wide = stream.astype(jnp.float32)
    normed = (
        wide
        * lax.rsqrt(jnp.mean(wide * wide, axis=-1, keepdims=True) + 1e-05)
        * gain.astype(jnp.float32)
    ).astype(jnp.bfloat16)
    tail = passed_along(normed[rows - (CONV - 1) :, :], "ctx", 1)
    padded = jnp.concatenate([tail, normed], axis=0)
    total = jnp.zeros((rows, width), jnp.float32)
    for offset in range(CONV):
        total = total + conv_taps[offset].astype(jnp.float32) * padded[
            offset : offset + rows
        ].astype(jnp.float32)
    mixed = jax.nn.silu(total).astype(jnp.bfloat16)
    count = rows // SPAN
    mixed_blocks = mixed.reshape(count, SPAN, HEADS, HEAD_DIM)
    write_blocks = writes.reshape(count, SPAN, GROUPS, STATE)
    read_blocks = reads.reshape(count, SPAN, GROUPS, STATE)
    step_blocks = jnp.transpose(steps.reshape(HEADS, count, SPAN), (1, 0, 2))
    decay_blocks = jnp.transpose(decays.reshape(HEADS, count, SPAN), (1, 0, 2))
    inner, factor, summary, cumul = jax.vmap(block_parts)(
        mixed_blocks, write_blocks, read_blocks, step_blocks, decay_blocks
    )
    own_factor = factor[0]
    own_state = summary[0]
    identity = (jnp.ones((HEADS,), jnp.float32), jnp.zeros((HEADS, STATE, HEAD_DIM), jnp.float32))
    _, entering = entering_2((own_factor, own_state), "ctx", combine, identity)
    entries = [entering.astype(jnp.bfloat16)]
    entries = jnp.stack(entries, axis=0)
    carried = jax.vmap(carried_term)(read_blocks, cumul, entries)
    skipped = skip[None, None, :, None] * mixed_blocks.astype(jnp.float32)
    result = (inner + carried + skipped).reshape(rows, width)
    return (wide + result).astype(jnp.bfloat16)


def shards(
    section_input, norm_gain, conv_weight, state_write, state_read, step_size, log_decay, skip_gain
):
    output = layer_body(
        section_input[0],
        norm_gain[0],
        conv_weight[0],
        state_write[0],
        state_read[0],
        step_size[0],
        log_decay[0],
        skip_gain[0],
    )
    handed = from_behind(output, "section", 1)
    return handed[None]


def solution(mesh):
    in_specs = (
        P("section", "ctx", None),
        P("section", None),
        P("section", None, None),
        P("section", "ctx", None),
        P("section", "ctx", None),
        P("section", None, "ctx"),
        P("section", None, "ctx"),
        P("section", None),
    )
    out_specs = P("section", "ctx", None)
    return jax.shard_map(shards, mesh=mesh, in_specs=in_specs, out_specs=out_specs, check_vma=False)
```

profile of v0, /device:TPU:96, one launch (start us, length us, event | category | flops | bytes accessed | tf_op | source)
XLA Modules:
  0.0 1608.0 jit_solution(17615479593969828426)
XLA Ops:
  29.8 12.1 fusion.20
  50.7 39.1 %all-gather = f32[32,128,1]{1,2,0:T(1,128)S(1)} all-gather(f32[1,128,1]{1,2,0:T(1,128)S(1)} %get-tuple-element.138), channel_id=2, replica_groups=mesh['section'=8,'ctx'=32] {'ctx'}, dimensions={0}, use_global_device_ids=true | all-gather | bytes 16896 | tf_op jit(solution)/shard_map/all_gather | solution.py:22
  89.8 783.1 %all-gather.3.cloned.1.call-done = f32[32,128,128,64]{2,3,1,0:T(8,128)} async-done(((f32[1,128,128,64]{2,3,1,0:T(8,128)}), f32[32,128,128,64]{2,3,1,0:T(8,128)}) %all-gather.3.cloned.1.call-update) | async-done | bytes 134217744 | tf_op jit(solution)/shard_map/all_gather | solution.py:22
  873.0 687.2 %while.14 = (s32[]{:T(128)}, f32[128,128,64]{2,1,0:T(8,128)}, s32[]{:T(128)}, f32[32,128]{1,0:T(8,128)S(1)}, f32[32,128,128,64]{2,3,1,0:T(8,128)}, /*index=5*/s32[]{:T(128)}, s32[]{:T(128)}) while((s32[]{:T(128)}, f32[128,128,64]{2,1,0:T(8,128)}, s32[]{:T(128)}, f32[32,128]{1,0:T(8,128)S(1)}, f32[32,128,128,64]{2,3,1,0:T(8,128)}, ...), condition=%wide.region_3.4_spmd.clone, body=%wide.region_2.3_spmd.clone.sunk | while | flops 4194308 | bytes 29361768 | solution.py:34
  877.7 6.9 copy.74
  895.4 6.9 copy.74
  902.3 10.0 fusion.25
  923.8 10.0 fusion.25
  938.6 6.9 copy.74
  945.4 10.0 fusion.25
  960.2 6.9 copy.74
  967.0 10.0 fusion.25
  981.8 6.9 copy.74
  988.6 10.0 fusion.25
  1003.4 6.9 copy.74
  1010.2 10.0 fusion.25
  1025.0 6.9 copy.74
  1031.8 10.0 fusion.25
  1046.6 6.9 copy.74
  1053.4 10.0 fusion.25
  1075.0 10.0 fusion.25
  1089.8 6.9 copy.74
  1096.6 10.0 fusion.25
  1111.4 6.9 copy.74
  1118.2 10.0 fusion.25
  1133.0 6.9 copy.74
  1139.8 10.0 fusion.25
  1154.5 6.9 copy.74
  1161.4 10.0 fusion.25
  1176.1 6.9 copy.74
  1183.0 10.0 fusion.25
  1197.7 6.9 copy.74
  1204.6 10.0 fusion.25
  1219.3 6.9 copy.74
  1226.2 10.0 fusion.25
  1240.9 6.9 copy.74
  1247.8 10.0 fusion.25
  1262.5 6.9 copy.74
  1269.4 10.0 fusion.25
  1284.1 6.9 copy.74
  1291.0 10.0 fusion.25
  1305.7 6.9 copy.74
  1312.6 10.0 fusion.25
  1334.2 10.0 fusion.25
  1348.9 6.9 copy.74
  1355.8 10.0 fusion.25
  1370.5 6.9 copy.74
  1377.4 10.0 fusion.25
  1392.1 6.9 copy.74
  1399.0 10.0 fusion.25
  1413.7 6.9 copy.74
  1420.6 10.0 fusion.25
  1435.3 6.9 copy.74
  1442.2 10.0 fusion.25
  1456.9 6.9 copy.74
  1463.8 10.0 fusion.25
  1485.4 10.0 fusion.25
  1500.1 6.9 copy.74
  1507.0 10.0 fusion.25
  1521.7 6.9 copy.74
  1528.6 10.0 fusion.25
  1543.3 6.9 copy.74
  1550.2 10.0 fusion.25
  1571.6 26.7 %collective-permute-done.1 = bf16[128,8192]{0,1:T(8,128)(2,1)S(1)} collective-permute-done((bf16[128,8192]{0,1:T(8,128)(2,1)S(1)}, bf16[128,8192]{0,1:T(8,128)(2,1)S(1)}, u32[]{:S(2)}, u32[]{:S(2)}) %collective-permute-start.1) | collective-permute-done | bytes 2097184 | tf_op jit(solution)/shard_map/ppermute | solution.py:40
  (127 shorter events, 231.2 us)
Async XLA Ops:
  6.5 4.3 copy-start.10
  6.5 866.4 %all-gather.3.cloned.1.call-start = ((), (), s32[]{:S(2)}) async-start(), calls=%async_computation | async-start | bytes 138412032 | tf_op jit(solution)/shard_map/all_gather | solution.py:22
  14.4 1.3 copy-start.2
  15.7 7.5 copy-start.8
  15.7 7.6 copy-start.9
  15.7 7.8 copy-start.5
  15.7 8.1 copy-start.6
  19.7 8.3 collective-permute-start
  41.9 3.2 copy-start
  45.2 0.9 copy-start.7
  1560.2 5.8 copy-start.4
  1564.7 2.2 copy-start.1
  1564.7 3.5 copy-start.3
  1564.7 3.5 copy-start.11
  1571.5 26.7 %collective-permute-start.1 = (bf16[128,8192]{0,1:T(8,128)(2,1)S(1)}, bf16[128,8192]{0,1:T(8,128)(2,1)S(1)}, u32[]{:S(2)}, u32[]{:S(2)}) collective-permute-start(bf16[128,8192]{0,1:T(8,128)(2,1)S(1)} %fusion.7), channel_id=1, source_target_pairs={{224,0},{0,32},{32,64},{64,96},{96,128},{128,160},{160,192},{192,2... | collective-permute-start | bytes 6291464 | tf_op jit(solution)/shard_map/ppermute | solution.py:40
Sparse Core Ops, SparseCore 0:
  45.3 827.5 all-gather.2
where the time goes:
time: 1610 us
  waiting for transfers between devices  814 us (51%)
  local copies, waits for them, and re-layouts  388 us (24%)
  other arithmetic  342 us (21%)
  blocking collectives  39.1 us (2%)
    all_gather x1, waiting for transfers between devices, entering_2(): everything = jax.tree.map(lambda part: lax.all_gather(part, axis), value)  783 us
    dynamic_slice x64, local copies, waits for them, and re-layouts, step(): new = combine(before, jax.tree.map(lambda part: part[k], everything))  371 us
    select_n x32, other arithmetic, step(): return jax.tree.map(lambda a, b: jnp.where(reached, a, b), new, before)  316 us
    all_gather x1, blocking collectives, entering_2(): everything = jax.tree.map(lambda part: lax.all_gather(part, axis), value)  39.1 us
  transfers between devices with their start and end apart: 3, of which 3 were waited for; matrix products, arithmetic and copies ran while one was open for 0% of the time, Pallas kernels for 0%

commit v1 on v0

v1 whole, which is shorter than its diff:
```python
import jax
import jax.numpy as jnp
from jax import lax
from jax.experimental import pallas as pl
from jax.experimental.pallas import tpu as pltpu
from jax.sharding import PartitionSpec as P

HEADS = 128
HEAD_DIM = 64
STATE = 128
GROUPS = 8
CONV = 4
SPAN = 128
WIDTH = HEADS * HEAD_DIM
RING = 4
LANES = 256
PAIRS = LANES // 128
CHUNK_HEADS = LANES // HEAD_DIM
CHUNKS = WIDTH // RING // LANES
GROUP_CHUNKS = WIDTH // GROUPS // LANES
LOG2E = 1.4426950408889634
F32 = jnp.float32
BF16 = jnp.bfloat16


def mixing_kernel(
    x_ref, gain_ref, taps_ref, write_ref, read_ref, step_ref, decay_ref, skip_ref,
    out_ref,
    padded, mixed, total, grown, scores, write_t, cum_cols, shift_rows, shift_cols, scale,
    halo_out, halo_in, end_out, end_in, sum_out, sum_in, state_in, state_out,
    back_out, back_in, last_out,
    halo_sem, end_sems, sum_sems, state_sems, back_sems, last_sems,
):
    sections, blocks = lax.axis_size("section"), lax.axis_size("ctx")
    rows = blocks // RING
    section, ctx = lax.axis_index("section"), lax.axis_index("ctx")
    row, place = ctx // RING, ctx % RING

    def at_ctx(index):
        return {"section": section, "ctx": index}

    def at_place(index):
        return at_ctx(row * RING + index)

    before_ctx, after_ctx = (ctx + blocks - 1) % blocks, (ctx + 1) % blocks
    before_section = {"section": (section + sections - 1) % sections, "ctx": ctx}
    after_section = {"section": (section + 1) % sections, "ctx": ctx}

    barrier = pltpu.get_barrier_semaphore()
    pl.semaphore_signal(barrier, 1, device_id=at_ctx(before_ctx))
    pl.semaphore_signal(barrier, 1, device_id=before_section)
    for distance in range(1, RING):
        pl.semaphore_signal(barrier, 1, device_id=at_place((place + distance) % RING))

    @pl.when(row > 0)
    def _():
        pl.semaphore_signal(barrier, 1, device_id=at_ctx(ctx - RING))

    def halo_copy():
        return pltpu.make_async_remote_copy(
            src_ref=halo_out, dst_ref=halo_in, send_sem=halo_sem.at[0], recv_sem=halo_sem.at[1],
            device_id=at_ctx(after_ctx),
        )

    def end_copy(to, slot):
        return pltpu.make_async_remote_copy(
            src_ref=end_out.at[to], dst_ref=end_in.at[slot],
            send_sem=end_sems.at[0, to], recv_sem=end_sems.at[1, slot], device_id=at_place(to),
        )

    def sum_copy(to, slot, j):
        return pltpu.make_async_remote_copy(
            src_ref=sum_out.at[to, j], dst_ref=sum_in.at[slot, j],
            send_sem=sum_sems.at[0, to, j], recv_sem=sum_sems.at[1, slot, j],
            device_id=at_place(to),
        )

    def state_copy(j):
        return pltpu.make_async_remote_copy(
            src_ref=state_out.at[j], dst_ref=state_in.at[j],
            send_sem=state_sems.at[0, j], recv_sem=state_sems.at[1, j],
            device_id=at_ctx((ctx + RING) % blocks),
        )

    def back_copy(to, slot, j):
        return pltpu.make_async_remote_copy(
            src_ref=back_out.at[to, j], dst_ref=back_in.at[slot, j],
            send_sem=back_sems.at[0, to, j], recv_sem=back_sems.at[1, slot, j],
            device_id=at_place(to),
        )

    def lanes_of(chunk):
        return pl.ds(pl.multiple_of(chunk * LANES, LANES), LANES)

    def last_copy(chunk):
        return pltpu.make_async_remote_copy(
            src_ref=last_out.at[chunk], dst_ref=out_ref.at[:, lanes_of(chunk)],
            send_sem=last_sems.at[0, chunk], recv_sem=last_sems.at[1, chunk],
            device_id=after_section,
        )

    def square_sum(first, count):
        def add(i, acc):
            part = x_ref[pl.ds(first, count), pl.ds(pl.multiple_of(i * 512, 512), 512)].astype(F32)
            part = part * part
            return acc + (
                (part[:, 0:128] + part[:, 128:256]) + (part[:, 256:384] + part[:, 384:512])
            )

        acc = lax.fori_loop(0, WIDTH // 512, add, jnp.zeros((count, 128), F32))
        mean = jnp.sum(acc, axis=-1, keepdims=True) * (1.0 / WIDTH)
        return jnp.broadcast_to(lax.rsqrt(mean + 1e-05), (count, 128))

    tail_scale = square_sum(SPAN - 16, 16)
    for i in range(8):
        span = slice(i * 1024, (i + 1) * 1024)
        wide = x_ref[SPAN - 16 : SPAN, span].astype(F32)
        normed = (wide * jnp.tile(tail_scale, (1, 8))) * gain_ref[:, span].astype(F32)
        normed = normed.astype(BF16).astype(F32)
        halo_out[3 * i : 3 * i + 3, :] = normed[13:16, :]

    pl.semaphore_wait(barrier, 1 + RING + jnp.where(row < rows - 1, 1, 0))

    halo_copy().start()

    token = lax.broadcasted_iota(jnp.int32, (SPAN, SPAN), 0)
    lane = lax.broadcasted_iota(jnp.int32, (SPAN, SPAN), 1)
    upper = jnp.where(token <= lane, 1.0, 0.0).astype(F32)
    cumul = lax.dot_general(
        decay_ref[...], upper, (((1,), (0,)), ((), ())),
        precision=lax.Precision.HIGHEST, preferred_element_type=F32,
    ) * LOG2E
    shift = cumul - jnp.log2(step_ref[...])
    shift_rows[...] = shift
    shift_cols[...] = shift.T
    cum_cols[...] = cumul.T
    low = lane < HEAD_DIM
    causal = token >= lane

    def columns(ref, chunk):
        return pltpu.roll(ref[...], (HEADS - chunk * CHUNK_HEADS) % HEADS, 1)

    def pair_of(cols, p):
        return jnp.where(
            low[: cols.shape[0]], cols[:, 2 * p : 2 * p + 1], cols[:, 2 * p + 1 : 2 * p + 2]
        )

    def put_ends(chunk, carry):
        cols = pltpu.roll(
            cum_cols[SPAN - 8 : SPAN, :], (HEADS - chunk * CHUNK_HEADS) % HEADS, 1
        )
        for p in range(PAIRS):
            pair = (chunk % CHUNKS) * PAIRS + p
            end_out[chunk // CHUNKS, pl.ds(pair, 1), :] = pair_of(cols, p)[7:8, :]
        return carry

    lax.fori_loop(0, RING * CHUNKS, put_ends, 0)
    for distance in range(1, RING):
        to = (place + distance) % RING
        end_copy(to, place).start()
    end_in[place] = end_out[place]

    scale[...] = square_sum(0, SPAN)

    def convolve(lanes, first, count):
        taps = taps_ref[:, lanes].astype(F32)
        acc = jnp.zeros((count, LANES), F32)
        for k in range(CONV):
            acc = acc + taps[k : k + 1, :] * padded[pl.ds(8 - (CONV - 1) + first + k, count), lanes]
        acc = acc * (0.5 + 0.5 * jnp.tanh(0.5 * acc))
        mixed[pl.ds(first, count), lanes] = acc.astype(BF16)

    def norm_chunk(i, carry):
        lanes = lanes_of(i)
        wide = x_ref[:, lanes].astype(F32)
        normed = (wide * jnp.tile(scale[...], (1, PAIRS))) * gain_ref[:, lanes].astype(F32)
        padded[pl.ds(8, SPAN), lanes] = normed.astype(BF16).astype(F32)
        convolve(lanes, 16, SPAN - 16)
        return carry

    lax.fori_loop(0, WIDTH // LANES, norm_chunk, 0)

    for g in range(GROUPS):
        span = slice(g * STATE, (g + 1) * STATE)
        writes = write_ref[:, span]
        scores[g] = lax.dot_general(
            read_ref[:, span], writes, (((1,), (1,)), ((), ())), preferred_element_type=F32
        )
        write_t[g] = writes.astype(F32).T.astype(BF16)

    halo_copy().wait()
    for i in range(8):
        rows3 = halo_in[3 * i : 3 * i + 3, :]
        padded[8 - (CONV - 1) : 8, i * 1024 : (i + 1) * 1024] = jnp.where(ctx > 0, rows3, 0.0)

    def first_rows(i, carry):
        convolve(lanes_of(i), 0, 16)
        return carry

    lax.fori_loop(0, WIDTH // LANES, first_rows, 0)

    def summarize(j, carry):
        def quarter(q, carry):
            chunk = q * CHUNKS + j
            lanes = lanes_of(chunk)
            cols = columns(shift_cols, chunk)
            parts = []
            for p in range(PAIRS):
                end = end_out[q, pl.ds(j * PAIRS + p, 1), :]
                parts.append(jnp.exp2(end - pair_of(cols, p)))
            scaled = (mixed[:, lanes].astype(F32) * jnp.concatenate(parts, axis=1)).astype(BF16)
            summary = jnp.dot(
                write_t[chunk // GROUP_CHUNKS], scaled, preferred_element_type=F32
            ).astype(BF16)
            sum_out[q, j] = summary

            @pl.when(q != place)
            def _():
                sum_copy(q, place, j).start()

            @pl.when(q == place)
            def _():
                sum_in[q, j] = summary

            return carry

        return lax.fori_loop(0, RING, quarter, carry)

    lax.fori_loop(0, CHUNKS, summarize, 0)

    for distance in range(1, RING):
        source = (place + distance) % RING
        end_copy(source, place).wait_send()
        end_copy(source, source).wait_recv()

    @pl.when(row == 0)
    def _():
        state_in[...] = jnp.zeros_like(state_in)

    def factor(source, j):
        return jnp.concatenate(
            [
                jnp.exp2(end_in[source, pl.ds(j * PAIRS + p, 1), :])
                for p in range(PAIRS)
            ],
            axis=1,
        )

    def relay(j):
        for distance in range(1, RING):
            source = (place + distance) % RING
            sum_copy(source, source, j).wait_recv()
        whole = factor(0, j)
        summed = sum_in[0, j].astype(F32)
        for block in range(1, RING):
            one = factor(block, j)
            whole = whole * one
            summed = summed * one + sum_in[block, j].astype(F32)

        @pl.when(row > 0)
        def _():
            state_copy(j).wait_recv()

        @pl.when(row < rows - 1)
        def _():
            entering = state_in[j].astype(F32)
            state_out[j] = (entering * whole + summed).astype(BF16)
            state_copy(j).start()

    def hand_back(j):
        state = state_in[j].astype(F32)
        back_out[0, j] = state_in[j]
        for block in range(1, RING):
            state = state * factor(block - 1, j) + sum_in[block - 1, j].astype(F32)
            back_out[block, j] = state.astype(BF16)
        for distance in range(1, RING):
            to = (place + distance) % RING
            back_copy(to, place, j).start()
        back_in[place, j] = back_out[place, j]

    def within(chunk, carry):
        lanes = lanes_of(chunk)
        score = scores[chunk // GROUP_CHUNKS]
        cols = columns(cum_cols, chunk)
        for p in range(PAIRS):
            at = pl.ds(pl.multiple_of(chunk * LANES + p * 128, 128), 128)
            weights = []
            spread = []
            for k in range(2):
                head = chunk * CHUNK_HEADS + 2 * p + k
                decay = jnp.broadcast_to(cols[:, 2 * p + k : 2 * p + k + 1], (SPAN, SPAN))
                spread.append(decay)
                weight = score * jnp.exp2(decay - shift_rows[pl.ds(head, 1), :])
                weights.append(jnp.where(causal, weight, 0.0).astype(BF16))
            both = mixed[:, at]
            nothing = jnp.zeros_like(both)
            apart = jnp.concatenate(
                [jnp.where(low, both, nothing), jnp.where(low, nothing, both)], axis=0
            )
            inner = jnp.dot(
                jnp.concatenate(weights, axis=1), apart, preferred_element_type=F32
            )
            head = chunk * CHUNK_HEADS + 2 * p
            skip = jnp.where(low[:1], skip_ref[0, head], skip_ref[0, head + 1])
            total[:, at] = x_ref[:, at].astype(F32) + inner + skip * both.astype(F32)
            grown[:, at] = jnp.exp2(jnp.where(low, spread[0], spread[1]))
        return carry

    def finish(j):
        for distance in range(1, RING):
            source = (place + distance) % RING
            back_copy(source, source, j).wait_recv()

        def quarter(q, carry):
            chunk = q * CHUNKS + j
            lanes = lanes_of(chunk)
            group = pl.ds(pl.multiple_of((chunk // GROUP_CHUNKS) * STATE, STATE), STATE)
            carried = jnp.dot(read_ref[:, group], back_in[q, j], preferred_element_type=F32)
            last_out[chunk] = (total[:, lanes] + grown[:, lanes] * carried).astype(BF16)
            last_copy(chunk).start()
            return carry

        lax.fori_loop(0, RING, quarter, 0)

    lag = jnp.maximum(rows - 1 - row, 0)
    ahead = jnp.minimum(row * 8, RING * CHUNKS)
    lax.fori_loop(0, ahead, within, 0)

    def pipeline(i, carry):
        @pl.when(i < CHUNKS)
        def _():
            relay(i)

        j = i - lag

        @pl.when((j >= 0) & (j < CHUNKS))
        def _():
            hand_back(j)

        return carry

    lax.fori_loop(0, lag, pipeline, 0)
    lax.fori_loop(ahead, RING * CHUNKS, within, 0)

    def pipeline_end(i, carry):
        pipeline(i, carry)
        j = i - lag - 1

        @pl.when(j >= 0)
        def _():
            finish(j)

        return carry

    lax.fori_loop(lag, lag + CHUNKS + 1, pipeline_end, 0)

    def settle(j, carry):
        for distance in range(1, RING):
            to = (place + distance) % RING
            sum_copy(to, place, j).wait_send()
            back_copy(to, place, j).wait_send()

        @pl.when(row < rows - 1)
        def _():
            state_copy(j).wait_send()

        for q in range(RING):
            last_copy(q * CHUNKS + j).wait()
        return carry

    lax.fori_loop(0, CHUNKS, settle, 0)


def shards(
    section_input, norm_gain, conv_weight, state_write, state_read, step_size, log_decay, skip_gain
):
    vmem = pl.BlockSpec(memory_space=pltpu.VMEM)
    dma = pltpu.SemaphoreType.DMA
    chunks = WIDTH // LANES
    half = (RING, CHUNKS, STATE, LANES)
    handed = pl.pallas_call(
        mixing_kernel,
        out_shape=jax.ShapeDtypeStruct((SPAN, WIDTH), BF16),
        in_specs=[vmem] * 7 + [pl.BlockSpec(memory_space=pltpu.SMEM)],
        out_specs=pl.BlockSpec(memory_space=pl.ANY),
        scratch_shapes=[
            pltpu.VMEM((SPAN + 8, WIDTH), F32),
            pltpu.VMEM((SPAN, WIDTH), BF16),
            pltpu.VMEM((SPAN, WIDTH), F32),
            pltpu.VMEM((SPAN, WIDTH), F32),
            pltpu.VMEM((GROUPS, SPAN, SPAN), F32),
            pltpu.VMEM((GROUPS, STATE, SPAN), BF16),
            pltpu.VMEM((SPAN, HEADS), F32),
            pltpu.VMEM((HEADS, SPAN), F32),
            pltpu.VMEM((SPAN, HEADS), F32),
            pltpu.VMEM((SPAN, 128), F32),
            pltpu.VMEM((24, 1024), F32),
            pltpu.VMEM((24, 1024), F32),
            pltpu.VMEM((RING, CHUNKS * PAIRS, 128), F32),
            pltpu.VMEM((RING, CHUNKS * PAIRS, 128), F32),
            pltpu.VMEM(half, BF16),
            pltpu.VMEM(half, BF16),
            pltpu.VMEM(half[1:], BF16),
            pltpu.VMEM(half[1:], BF16),
            pltpu.VMEM(half, BF16),
            pltpu.VMEM(half, BF16),
            pltpu.VMEM((chunks, SPAN, LANES), BF16),
            dma((2,)),
            dma((2, RING)),
            dma((2, RING, CHUNKS)),
            dma((2, CHUNKS)),
            dma((2, RING, CHUNKS)),
            dma((2, chunks)),
        ],
        compiler_params=pltpu.CompilerParams(
            collective_id=0, has_side_effects=True, vmem_limit_bytes=52 << 20
        ),
    )(
        section_input[0],
        norm_gain,
        conv_weight[0],
        state_write[0],
        state_read[0],
        step_size[0],
        log_decay[0],
        skip_gain,
    )
    return handed[None]


def solution(mesh):
    in_specs = (
        P("section", "ctx", None),
        P("section", None),
        P("section", None, None),
        P("section", "ctx", None),
        P("section", "ctx", None),
        P("section", None, "ctx"),
        P("section", None, "ctx"),
        P("section", None),
    )
    out_specs = P("section", "ctx", None)
    return jax.shard_map(shards, mesh=mesh, in_specs=in_specs, out_specs=out_specs, check_vma=False)
```

time: 1610 us -> 93.4 us (0.06)
  the two profiles are of different devices: /device:TPU:96 before, /device:TPU:1 now
where the time goes in v1:
time: 93.4 us; the launch traced here: 93 us
  Pallas kernels  84 us (90%)
  local copies, waits for them, and re-layouts  8.92 us (10%)
    pallas_call x1, Pallas kernels, shards(): pl.pallas_call(mixing_kernel, out_shape=jax.ShapeDtypeStruct((SPAN, WIDTH...  84 us
    unnamed x15, local copies, waits for them, and re-layouts  8.92 us

profile of v1, /device:TPU:1, one launch (start us, length us, event | category | flops | bytes accessed | tf_op | source)
XLA Modules:
  0.0 93.0 jit_solution(17555824496314708755)
XLA Ops:
  0.0 0.0 copy-start
  0.0 0.9 %copy-done = bf16[1,128,1024]{2,1,0:T(8,128)(2,1)S(1)} copy-done((bf16[1,128,1024]{2,1,0:T(8,128)(2,1)S(1)}, bf16[1,128,1024]{2,1,0:T(8,128)(2,1)}, u32[]{:S(2)}) %copy-start) | copy-done | bytes 262168
  1.0 0.0 copy-start.1
  1.0 0.9 %copy-done.1 = bf16[1,128,1024]{2,1,0:T(8,128)(2,1)S(1)} copy-done((bf16[1,128,1024]{2,1,0:T(8,128)(2,1)S(1)}, bf16[1,128,1024]{2,1,0:T(8,128)(2,1)}, u32[]{:S(2)}) %copy-start.1) | copy-done | bytes 262168
  1.9 0.0 copy-start.2
  1.9 0.8 copy-done.2
  2.7 0.0 copy-start.3
  2.7 0.8 copy-done.3
  3.6 0.0 copy-start.4
  3.6 0.8 copy-done.4
  4.4 0.0 copy-start.5
  4.4 0.8 copy-done.5
  5.2 0.0 copy-start.6
  5.2 0.7 copy-done.6
  5.8 84.0 %shard_map.82 = bf16[128,8192]{1,0:T(8,128)(2,1)} custom-call(bf16[128,8192]{1,0:T(8,128)(2,1)} %bitcast.13, bf16[1,8192]{1,0:T(2,128)(2,1)S(1)} %copy-done.5, bf16[4,8192]{1,0:T(4,128)(2,1)S(1)} %bitcast.9, bf16[128,1024]{1,0:T(8,128)(2,1)S(1)} %bitcast.7, bf16[128,1024]{1,0:T(8,128)(2,1)S(1)} %bitcast.8, f32[128,128]{1,0:T(8,128)S(1)} %bitcast.10, ...), custom_call_target="tpu_custom_call" | custom-call | tf_op jit(solution)/shard_map/pallas_call | solution.py:381
  89.9 3.1 %copy.10 = bf16[1,128,8192]{2,1,0:T(8,128)(2,1)} copy(bf16[1,128,8192]{2,1,0:T(8,128)(2,1)} %bitcast.12) | data formatting | bytes 4194304
Async XLA Ops:
  0.0 0.9 %copy-start = (bf16[1,128,1024]{2,1,0:T(8,128)(2,1)S(1)}, bf16[1,128,1024]{2,1,0:T(8,128)(2,1)}, u32[]{:S(2)}) copy-start(bf16[1,128,1024]{2,1,0:T(8,128)(2,1)} %param.11) | copy-start | bytes 786436
  1.0 0.9 %copy-start.1 = (bf16[1,128,1024]{2,1,0:T(8,128)(2,1)S(1)}, bf16[1,128,1024]{2,1,0:T(8,128)(2,1)}, u32[]{:S(2)}) copy-start(bf16[1,128,1024]{2,1,0:T(8,128)(2,1)} %param.12) | copy-start | bytes 786436
  1.9 0.8 copy-start.2
  2.7 0.8 copy-start.3
  3.6 0.8 copy-start.4
  4.4 0.8 copy-start.5
  5.2 0.7 copy-start.6

commit v2 on v1

v2 whole, which is shorter than its diff:
```python
import jax
import jax.numpy as jnp
from jax import lax
from jax.experimental import pallas as pl
from jax.experimental.pallas import tpu as pltpu
from jax.sharding import PartitionSpec as P

HEADS = 128
HEAD_DIM = 64
STATE = 128
GROUPS = 8
CONV = 4
SPAN = 128
WIDTH = HEADS * HEAD_DIM
RING = 4
LANES = 256
PAIRS = LANES // 128
CHUNK_HEADS = LANES // HEAD_DIM
CHUNKS = WIDTH // RING // LANES
GROUP_CHUNKS = WIDTH // GROUPS // LANES
LOG2E = 1.4426950408889634
F32 = jnp.float32
BF16 = jnp.bfloat16


def mixing_kernel(
    x_hbm, gain_hbm, taps_hbm, write_hbm, read_hbm, step_hbm, decay_hbm, skip_ref,
    out_ref,
    x_ref, gain_ref, taps_ref, write_ref, read_ref, step_ref, decay_ref,
    scale_buf, padded, mixed, total, grown, scores, write_t, cum_rows, cum_cols, shift_rows, shift_cols,
    halo_out, halo_in, end_out, end_in, sum_out, sum_in, state_in, state_out,
    back_out, back_in, last_out,
    fetch_sems, halo_sems, end_sems, sum_sems, state_sems, back_sems, last_sems,
):
    sections, blocks = lax.axis_size("section"), lax.axis_size("ctx")
    rows = blocks // RING
    section, ctx = lax.axis_index("section"), lax.axis_index("ctx")
    row, place = ctx // RING, ctx % RING

    def at_ctx(index):
        return {"section": section, "ctx": index}

    def at_place(index):
        return at_ctx(row * RING + index)

    before_ctx, after_ctx = (ctx + blocks - 1) % blocks, (ctx + 1) % blocks
    before_section = {"section": (section + sections - 1) % sections, "ctx": ctx}
    after_section = {"section": (section + 1) % sections, "ctx": ctx}

    late = SPAN - 16
    fetches = [
        pltpu.make_async_copy(source, target, fetch_sems.at[i])
        for i, (source, target) in enumerate(
            [
                (x_hbm.at[pl.ds(late, 16)], x_ref.at[pl.ds(late, 16)]),
                (gain_hbm, gain_ref),
                (decay_hbm, decay_ref),
                (step_hbm, step_ref),
                (x_hbm.at[pl.ds(0, late)], x_ref.at[pl.ds(0, late)]),
                (taps_hbm, taps_ref),
                (write_hbm, write_ref),
                (read_hbm, read_ref),
            ]
        )
    ]
    for fetch in fetches:
        fetch.start()

    barrier = pltpu.get_barrier_semaphore()
    pl.semaphore_signal(barrier, 1, device_id=before_section)
    for distance in range(1, RING):
        pl.semaphore_signal(barrier, 1, device_id=at_place((place + distance) % RING))

    @pl.when(ctx > 0)
    def _():
        pl.semaphore_signal(barrier, 1, device_id=at_ctx(before_ctx))

    @pl.when(row > 0)
    def _():
        pl.semaphore_signal(barrier, 1, device_id=at_ctx(ctx - RING))

    def halo_copy(j):
        return pltpu.make_async_remote_copy(
            src_ref=halo_out.at[j], dst_ref=halo_in.at[j],
            send_sem=halo_sems.at[0, j], recv_sem=halo_sems.at[1, j],
            device_id=at_ctx(after_ctx),
        )

    def end_copy(to, slot):
        return pltpu.make_async_remote_copy(
            src_ref=end_out.at[to], dst_ref=end_in.at[slot],
            send_sem=end_sems.at[0, to], recv_sem=end_sems.at[1, slot], device_id=at_place(to),
        )

    def sum_copy(to, slot, j):
        return pltpu.make_async_remote_copy(
            src_ref=sum_out.at[to, j], dst_ref=sum_in.at[slot, j],
            send_sem=sum_sems.at[0, to, j], recv_sem=sum_sems.at[1, slot, j],
            device_id=at_place(to),
        )

    def state_copy(j):
        return pltpu.make_async_remote_copy(
            src_ref=state_out.at[j], dst_ref=state_in.at[j],
            send_sem=state_sems.at[0, j], recv_sem=state_sems.at[1, j],
            device_id=at_ctx((ctx + RING) % blocks),
        )

    def back_copy(to, slot, j):
        return pltpu.make_async_remote_copy(
            src_ref=back_out.at[to, j], dst_ref=back_in.at[slot, j],
            send_sem=back_sems.at[0, to, j], recv_sem=back_sems.at[1, slot, j],
            device_id=at_place(to),
        )

    def lanes_of(chunk):
        return pl.ds(pl.multiple_of(chunk * LANES, LANES), LANES)

    def last_copy(chunk):
        return pltpu.make_async_remote_copy(
            src_ref=last_out.at[chunk], dst_ref=out_ref.at[:, lanes_of(chunk)],
            send_sem=last_sems.at[0, chunk], recv_sem=last_sems.at[1, chunk],
            device_id=after_section,
        )

    def square_sum(first, count):
        def add(i, acc):
            part = x_ref[pl.ds(first, count), pl.ds(pl.multiple_of(i * 1024, 1024), 1024)]
            for k in range(8):
                piece = part[:, k * 128 : (k + 1) * 128].astype(F32)
                acc = acc + piece * piece
            return acc

        acc = lax.fori_loop(0, WIDTH // 1024, add, jnp.zeros((count, 128), F32))
        mean = jnp.sum(acc, axis=-1, keepdims=True) * (1.0 / WIDTH)
        return jnp.broadcast_to(lax.rsqrt(mean + 1e-05), (count, 128))

    fetches[0].wait()
    fetches[1].wait()
    tail_scale = square_sum(late, 16)
    for chunk in range(RING * CHUNKS):
        for p in range(PAIRS):
            span = slice(chunk * LANES + p * 128, chunk * LANES + p * 128 + 128)
            normed = (x_ref[late:SPAN, span].astype(F32) * tail_scale) * gain_ref[:, span].astype(F32)
            normed = normed.astype(BF16).astype(F32)
            halo_out[chunk % CHUNKS, chunk // CHUNKS, 4 * p : 4 * p + 3, :] = normed[13:16, :]

    pl.semaphore_wait(
        barrier, RING + jnp.where(ctx < blocks - 1, 1, 0) + jnp.where(row < rows - 1, 1, 0)
    )

    @pl.when(ctx < blocks - 1)
    def _():
        for j in range(CHUNKS):
            halo_copy(j).start()

    @pl.when(ctx == 0)
    def _():
        halo_in[...] = jnp.zeros_like(halo_in)

    token = lax.broadcasted_iota(jnp.int32, (SPAN, SPAN), 0)
    lane = lax.broadcasted_iota(jnp.int32, (SPAN, SPAN), 1)
    low = lane < HEAD_DIM
    causal = token >= lane
    upper = jnp.where(token <= lane, 1.0, 0.0).astype(F32)
    fetches[2].wait()
    cumul = lax.dot_general(
        decay_ref[...], upper, (((1,), (0,)), ((), ())),
        precision=lax.Precision.HIGHEST, preferred_element_type=F32,
    ) * LOG2E
    cum_rows[...] = cumul
    even, odd = (
        jnp.broadcast_to(cum_rows[pl.ds(first, HEADS // 2, stride=2), :][:, SPAN - 1 :], (HEADS // 2, 128))
        for first in range(2)
    )
    end_out[...] = jnp.where(low[: HEADS // 2], even, odd).reshape(RING, CHUNKS * PAIRS, 128)
    for distance in range(1, RING):
        to = (place + distance) % RING
        end_copy(to, place).start()
    end_in[place] = end_out[place]
    cum_cols[...] = cumul.T
    fetches[3].wait()
    shift = cumul - jnp.log2(step_ref[...])
    shift_rows[...] = shift
    shift_cols[...] = shift.T

    fetches[4].wait()
    scale = square_sum(0, SPAN)
    for fetch in fetches[5:]:
        fetch.wait()

    for g in range(GROUPS):
        span = slice(g * STATE, (g + 1) * STATE)
        writes = write_ref[:, span]
        scores[g] = lax.dot_general(
            read_ref[:, span], writes, (((1,), (1,)), ((), ())), preferred_element_type=F32
        )
        write_t[g] = writes.astype(F32).T.astype(BF16)

    def columns(ref, j):
        return pltpu.roll(ref[...], (HEADS - j * CHUNK_HEADS) % HEADS, 1)

    def pair_lanes(chunk, p):
        return pl.ds(pl.multiple_of(chunk * LANES + p * 128, 128), 128)

    scale_buf[...] = scale

    def produce(j):
        @pl.when(ctx > 0)
        def _():
            halo_copy(j).wait_recv()

        cols = columns(shift_cols, j)
        for q in range(RING):
            chunk = q * CHUNKS + j
            parts = []
            for p in range(PAIRS):
                at = pair_lanes(chunk, p)
                buffer = padded.at[q * PAIRS + p]
                normed = (x_ref[:, at].astype(F32) * scale_buf[...]) * gain_ref[:, at].astype(F32)
                buffer[8:, :] = normed.astype(BF16).astype(F32)
                buffer[8 - (CONV - 1) : 8, :] = halo_in[j, q, 4 * p : 4 * p + 3, :]
                taps = taps_ref[:, at].astype(F32)
                acc = taps[0:1, :] * buffer[8 - (CONV - 1) : 8 - (CONV - 1) + SPAN, :]
                for k in range(1, CONV):
                    first = 8 - (CONV - 1) + k
                    acc = acc + taps[k : k + 1, :] * buffer[first : first + SPAN, :]
                acc = acc * (0.5 + 0.5 * jnp.tanh(0.5 * acc))
                value = acc.astype(BF16)
                mixed[:, at] = value
                head = q * (HEADS // RING) + 2 * p
                spread = jnp.where(low, cols[:, head : head + 1], cols[:, head + 1 : head + 2])
                end = end_out[q, pl.ds(j * PAIRS + p, 1), :]
                parts.append((value.astype(F32) * jnp.exp2(end - spread)).astype(BF16))
            sum_out[q, j] = jnp.dot(
                write_t[chunk // GROUP_CHUNKS],
                jnp.concatenate(parts, axis=1),
                preferred_element_type=F32,
            ).astype(BF16)
        for distance in (2, 1, 3):
            sum_copy((place + distance) % RING, place, j).start()
        sum_in[place, j] = sum_out[place, j]

    @pl.when(row == 0)
    def _():
        state_in[...] = jnp.zeros_like(state_in)

    def factor(source, j):
        return jnp.concatenate(
            [jnp.exp2(end_in[source, pl.ds(j * PAIRS + p, 1), :]) for p in range(PAIRS)], axis=1
        )

    def relay(j):
        for distance in range(1, RING):
            source = (place + distance) % RING
            sum_copy(source, source, j).wait_recv()
        whole = factor(0, j)
        summed = sum_in[0, j].astype(F32)
        for block in range(1, RING):
            one = factor(block, j)
            whole = whole * one
            summed = summed * one + sum_in[block, j].astype(F32)

        @pl.when(row > 0)
        def _():
            state_copy(j).wait_recv()

        @pl.when(row < rows - 1)
        def _():
            entering = state_in[j].astype(F32)
            state_out[j] = (entering * whole + summed).astype(BF16)
            state_copy(j).start()

    def hand_back(j):
        state = state_in[j].astype(F32)
        back_out[0, j] = state_in[j]
        for block in range(1, RING):
            state = state * factor(block - 1, j) + sum_in[block - 1, j].astype(F32)
            back_out[block, j] = state.astype(BF16)
        for distance in range(1, RING):
            to = (place + distance) % RING
            back_copy(to, place, j).start()
        back_in[place, j] = back_out[place, j]

    def within(j):
        cols = columns(cum_cols, j)
        for q in range(RING):
            chunk = q * CHUNKS + j
            score = scores[chunk // GROUP_CHUNKS]
            for p in range(PAIRS):
                at = pair_lanes(chunk, p)
                weights = []
                spread = []
                for k in range(2):
                    lane_at = q * (HEADS // RING) + 2 * p + k
                    decay = jnp.broadcast_to(cols[:, lane_at : lane_at + 1], (SPAN, SPAN))
                    spread.append(decay)
                    row_at = pl.ds(chunk * CHUNK_HEADS + 2 * p + k, 1)
                    weight = score * jnp.exp2(decay - shift_rows[row_at, :])
                    weights.append(jnp.where(causal, weight, 0.0).astype(BF16))
                both = mixed[:, at]
                nothing = jnp.zeros_like(both)
                apart = jnp.concatenate(
                    [jnp.where(low, both, nothing), jnp.where(low, nothing, both)], axis=0
                )
                inner = jnp.dot(
                    jnp.concatenate(weights, axis=1), apart, preferred_element_type=F32
                )
                head = chunk * CHUNK_HEADS + 2 * p
                skip = jnp.where(low[:1], skip_ref[0, head], skip_ref[0, head + 1])
                total[:, at] = x_ref[:, at].astype(F32) + inner + skip * both.astype(F32)
                grown[:, at] = jnp.exp2(jnp.where(low, spread[0], spread[1]))

    def finish(j):
        for distance in range(1, RING):
            source = (place + distance) % RING
            back_copy(source, source, j).wait_recv()
        for q in range(RING):
            chunk = q * CHUNKS + j
            lanes = lanes_of(chunk)
            group = pl.ds(pl.multiple_of((chunk // GROUP_CHUNKS) * STATE, STATE), STATE)
            carried = jnp.dot(read_ref[:, group], back_in[q, j], preferred_element_type=F32)
            last_out[chunk] = (total[:, lanes] + grown[:, lanes] * carried).astype(BF16)
        for q in range(RING):
            last_copy(q * CHUNKS + j).start()

    early = jnp.where(row == 0, 3, 0)
    begun = CHUNKS - early

    def first_steps(i, carry):
        produce(i)

        @pl.when(i == 0)
        def _():
            for distance in range(1, RING):
                source = (place + distance) % RING
                end_copy(source, place).wait_send()
                end_copy(source, source).wait_recv()

        @pl.when(i >= begun)
        def _():
            relay(i - begun)

        return carry

    lax.fori_loop(0, CHUNKS, first_steps, 0)

    def only_within(i, carry):
        within(i)
        return carry

    ahead = jnp.clip(5 * row - 4, 0, CHUNKS)
    lax.fori_loop(0, ahead, only_within, 0)
    lag = jnp.maximum(rows - 1 - row, 0)

    def last_steps(i, carry):
        @pl.when(i < CHUNKS)
        def _():
            relay(i)

        j = i - lag

        @pl.when((j >= 0) & (j < CHUNKS))
        def _():
            hand_back(j)

        piece = ahead + i - early

        @pl.when(piece < CHUNKS)
        def _():
            within(piece)

        @pl.when(j >= 1)
        def _():
            finish(j - 1)

        return carry

    lax.fori_loop(early, lag + CHUNKS + 1, last_steps, 0)

    def settle(j, carry):
        for distance in range(1, RING):
            to = (place + distance) % RING
            sum_copy(to, place, j).wait_send()
            back_copy(to, place, j).wait_send()

        @pl.when(ctx < blocks - 1)
        def _():
            halo_copy(j).wait_send()

        @pl.when(row < rows - 1)
        def _():
            state_copy(j).wait_send()

        for q in range(RING):
            last_copy(q * CHUNKS + j).wait()
        return carry

    lax.fori_loop(0, CHUNKS, settle, 0)


def shards(
    section_input, norm_gain, conv_weight, state_write, state_read, step_size, log_decay, skip_gain
):
    hbm = pl.BlockSpec(memory_space=pltpu.HBM)
    dma = pltpu.SemaphoreType.DMA
    chunks = WIDTH // LANES
    half = (RING, CHUNKS, STATE, LANES)
    halo = (CHUNKS, RING, 8, 128)
    handed = pl.pallas_call(
        mixing_kernel,
        out_shape=jax.ShapeDtypeStruct((SPAN, WIDTH), BF16),
        in_specs=[hbm] * 7 + [pl.BlockSpec(memory_space=pltpu.SMEM)],
        out_specs=pl.BlockSpec(memory_space=pltpu.VMEM),
        scratch_shapes=[
            pltpu.VMEM((SPAN, WIDTH), BF16),
            pltpu.VMEM((1, WIDTH), BF16),
            pltpu.VMEM((CONV, WIDTH), BF16),
            pltpu.VMEM((SPAN, GROUPS * STATE), BF16),
            pltpu.VMEM((SPAN, GROUPS * STATE), BF16),
            pltpu.VMEM((HEADS, SPAN), F32),
            pltpu.VMEM((HEADS, SPAN), F32),
            pltpu.VMEM((SPAN, 128), F32),
            pltpu.VMEM((RING * PAIRS, SPAN + 8, 128), F32),
            pltpu.VMEM((SPAN, WIDTH), BF16),
            pltpu.VMEM((SPAN, WIDTH), F32),
            pltpu.VMEM((SPAN, WIDTH), F32),
            pltpu.VMEM((GROUPS, SPAN, SPAN), F32),
            pltpu.VMEM((GROUPS, STATE, SPAN), BF16),
            pltpu.VMEM((HEADS, SPAN), F32),
            pltpu.VMEM((SPAN, HEADS), F32),
            pltpu.VMEM((HEADS, SPAN), F32),
            pltpu.VMEM((SPAN, HEADS), F32),
            pltpu.VMEM(halo, F32),
            pltpu.VMEM(halo, F32),
            pltpu.VMEM((RING, CHUNKS * PAIRS, 128), F32),
            pltpu.VMEM((RING, CHUNKS * PAIRS, 128), F32),
            pltpu.VMEM(half, BF16),
            pltpu.VMEM(half, BF16),
            pltpu.VMEM(half[1:], BF16),
            pltpu.VMEM(half[1:], BF16),
            pltpu.VMEM(half, BF16),
            pltpu.VMEM(half, BF16),
            pltpu.VMEM((chunks, SPAN, LANES), BF16),
            dma((8,)),
            dma((2, CHUNKS)),
            dma((2, RING)),
            dma((2, RING, CHUNKS)),
            dma((2, CHUNKS)),
            dma((2, RING, CHUNKS)),
            dma((2, chunks)),
        ],
        compiler_params=pltpu.CompilerParams(
            collective_id=0, has_side_effects=True, vmem_limit_bytes=48 << 20
        ),
    )(
        *(
            pltpu.with_memory_space_constraint(operand, pltpu.HBM)
            for operand in (
                section_input[0],
                norm_gain,
                conv_weight[0],
                state_write[0],
                state_read[0],
                step_size[0],
                log_decay[0],
            )
        ),
        skip_gain,
    )
    return handed[None]


def solution(mesh):
    in_specs = (
        P("section", "ctx", None),
        P("section", None),
        P("section", None, None),
        P("section", "ctx", None),
        P("section", "ctx", None),
        P("section", None, "ctx"),
        P("section", None, "ctx"),
        P("section", None),
    )
    out_specs = P("section", "ctx", None)
    return jax.shard_map(shards, mesh=mesh, in_specs=in_specs, out_specs=out_specs, check_vma=False)
```

time: 93.4 us -> 67.2 us (0.72)
  the two profiles are of different devices: /device:TPU:1 before, /device:TPU:225 now
where the time goes in v2:
time: 67.2 us; the launch traced here: 67.1 us
  Pallas kernels  65.1 us (97%)
  local copies, waits for them, and re-layouts  1.98 us (3%)
    pallas_call x1, Pallas kernels, shards(): pl.pallas_call(mixing_kernel, out_shape=jax.ShapeDtypeStruct((SPAN, WIDTH...  65.1 us
    unnamed x3, local copies, waits for them, and re-layouts  1.98 us

profile of v2, /device:TPU:225, one launch (start us, length us, event | category | flops | bytes accessed | tf_op | source)
XLA Modules:
  0.0 67.1 jit_solution(13621480907366935452)
XLA Ops:
  0.0 0.0 copy-start
  0.0 0.7 copy-done
  0.7 65.1 %shard_map.82 = bf16[128,8192]{1,0:T(8,128)(2,1)S(1)} custom-call(bf16[128,8192]{1,0:T(8,128)(2,1)} %bitcast.8, bf16[1,8192]{1,0:T(2,128)(2,1)} %gain_hbm.1, bf16[4,8192]{1,0:T(4,128)(2,1)} %bitcast.11, bf16[128,1024]{1,0:T(8,128)(2,1)} %bitcast.9, bf16[128,1024]{1,0:T(8,128)(2,1)} %bitcast.10, f32[128,128]{1,0:T(8,128)} %bitcast.12, f32[128,128]{1,0:T(8,128)} %bitcast.13, ...), custom_call_target="tpu_custom_call" | custom-call | tf_op jit(solution)/shard_map/pallas_call | solution.py:410
  65.7 1.3 %copy.10 = bf16[1,128,8192]{2,1,0:T(8,128)(2,1)} copy(bf16[1,128,8192]{2,1,0:T(8,128)(2,1)S(1)} %bitcast.7) | data formatting | bytes 4194304
Async XLA Ops:
  0.0 0.7 copy-start

commit v3 on v2

--- a/solution.py
+++ b/solution.py
@@ -18,6 +18,10 @@
 CHUNK_HEADS = LANES // HEAD_DIM
 CHUNKS = WIDTH // RING // LANES
 GROUP_CHUNKS = WIDTH // GROUPS // LANES
+LATER = 3
+EVEN = 3
+ODD = 3
+LAG = 5
 LOG2E = 1.4426950408889634
 F32 = jnp.float32
 BF16 = jnp.bfloat16
@@ -27,15 +31,18 @@
     x_hbm, gain_hbm, taps_hbm, write_hbm, read_hbm, step_hbm, decay_hbm, skip_ref,
     out_ref,
     x_ref, gain_ref, taps_ref, write_ref, read_ref, step_ref, decay_ref,
-    scale_buf, padded, mixed, total, grown, scores, write_t, cum_rows, cum_cols, shift_rows, shift_cols,
+    scale_buf, padded, mixed, grown, scores, write_t, cum_rows, cum_cols, shift_rows, shift_cols,
     halo_out, halo_in, end_out, end_in, sum_out, sum_in, state_in, state_out,
-    back_out, back_in, last_out,
-    fetch_sems, halo_sems, end_sems, sum_sems, state_sems, back_sems, last_sems,
+    front_out, front_in, fade_out, fade_in,
+    back_out, back_in, part_out, part_in, read_in, cum_in,
+    fetch_sems, halo_sems, end_sems, sum_sems, state_sems, front_sems, fade_sems, back_sems, part_sems, map_sems,
 ):
     sections, blocks = lax.axis_size("section"), lax.axis_size("ctx")
     rows = blocks // RING
     section, ctx = lax.axis_index("section"), lax.axis_index("ctx")
     row, place = ctx // RING, ctx % RING
+    second = row % 2 == 1
+    passes_on = second & (row < rows - 1)
 
     def at_ctx(index):
         return {"section": section, "ctx": index}
@@ -44,8 +51,10 @@
         return at_ctx(row * RING + index)
 
     before_ctx, after_ctx = (ctx + blocks - 1) % blocks, (ctx + 1) % blocks
-    before_section = {"section": (section + sections - 1) % sections, "ctx": ctx}
-    after_section = {"section": (section + 1) % sections, "ctx": ctx}
+    before_section, after_section = (section + sections - 1) % sections, (section + 1) % sections
+
+    def next_layer(index):
+        return {"section": after_section, "ctx": row * RING + index}
 
     late = SPAN - 16
     fetches = [
@@ -67,7 +76,9 @@
         fetch.start()
 
     barrier = pltpu.get_barrier_semaphore()
-    pl.semaphore_signal(barrier, 1, device_id=before_section)
+    for index in range(RING):
+        holder = {"section": before_section, "ctx": row * RING + index}
+        pl.semaphore_signal(barrier, 1, device_id=holder)
     for distance in range(1, RING):
         pl.semaphore_signal(barrier, 1, device_id=at_place((place + distance) % RING))
 
@@ -78,6 +89,10 @@
     @pl.when(row > 0)
     def _():
         pl.semaphore_signal(barrier, 1, device_id=at_ctx(ctx - RING))
+
+    @pl.when(second & (row > 1))
+    def _():
+        pl.semaphore_signal(barrier, 1, device_id=at_ctx(ctx - 2 * RING))
 
     def halo_copy(j):
         return pltpu.make_async_remote_copy(
@@ -99,10 +114,23 @@
             device_id=at_place(to),
         )
 
-    def state_copy(j):
+    def state_copy(j, hops):
         return pltpu.make_async_remote_copy(
             src_ref=state_out.at[j], dst_ref=state_in.at[j],
-            send_sem=state_sems.at[0, j], recv_sem=state_sems.at[1, j],
+            send_sem=state_sems.at[hops, j], recv_sem=state_sems.at[0, j],
+            device_id=at_ctx((ctx + hops * RING) % blocks),
+        )
+
+    def front_copy(j):
+        return pltpu.make_async_remote_copy(
+            src_ref=front_out.at[j], dst_ref=front_in.at[j],
+            send_sem=front_sems.at[0, j], recv_sem=front_sems.at[1, j],
+            device_id=at_ctx((ctx + RING) % blocks),
+        )
+
+    def fade_copy():
+        return pltpu.make_async_remote_copy(
+            src_ref=fade_out, dst_ref=fade_in, send_sem=fade_sems.at[0], recv_sem=fade_sems.at[1],
             device_id=at_ctx((ctx + RING) % blocks),
         )
 
@@ -110,18 +138,29 @@
         return pltpu.make_async_remote_copy(
             src_ref=back_out.at[to, j], dst_ref=back_in.at[slot, j],
             send_sem=back_sems.at[0, to, j], recv_sem=back_sems.at[1, slot, j],
-            device_id=at_place(to),
+            device_id=next_layer(to),
         )
 
     def lanes_of(chunk):
         return pl.ds(pl.multiple_of(chunk * LANES, LANES), LANES)
 
-    def last_copy(chunk):
-        return pltpu.make_async_remote_copy(
-            src_ref=last_out.at[chunk], dst_ref=out_ref.at[:, lanes_of(chunk)],
-            send_sem=last_sems.at[0, chunk], recv_sem=last_sems.at[1, chunk],
-            device_id=after_section,
-        )
+    def part_copy(chunk):
+        return pltpu.make_async_remote_copy(
+            src_ref=part_out.at[chunk], dst_ref=part_in.at[chunk],
+            send_sem=part_sems.at[0, chunk], recv_sem=part_sems.at[1, chunk],
+            device_id=next_layer(place),
+        )
+
+    def map_copies(*which):
+        return [
+            pltpu.make_async_remote_copy(
+                src_ref=source, dst_ref=target,
+                send_sem=map_sems.at[0, i], recv_sem=map_sems.at[1, i],
+                device_id=next_layer(place),
+            )
+            for i, (source, target) in enumerate([(cum_cols, cum_in), (read_ref, read_in)])
+            if i in which
+        ]
 
     def square_sum(first, count):
         def add(i, acc):
@@ -146,7 +185,10 @@
             halo_out[chunk % CHUNKS, chunk // CHUNKS, 4 * p : 4 * p + 3, :] = normed[13:16, :]
 
     pl.semaphore_wait(
-        barrier, RING + jnp.where(ctx < blocks - 1, 1, 0) + jnp.where(row < rows - 1, 1, 0)
+        barrier,
+        2 * RING - 1
+        + jnp.where(ctx < blocks - 1, 1, 0)
+        + jnp.where(second, jnp.where(row < rows - 1, 2, 0), 1),
     )
 
     @pl.when(ctx < blocks - 1)
@@ -179,6 +221,7 @@
         end_copy(to, place).start()
     end_in[place] = end_out[place]
     cum_cols[...] = cumul.T
+    map_copies(0)[0].start()
     fetches[3].wait()
     shift = cumul - jnp.log2(step_ref[...])
     shift_rows[...] = shift
@@ -188,6 +231,7 @@
     scale = square_sum(0, SPAN)
     for fetch in fetches[5:]:
         fetch.wait()
+    map_copies(1)[0].start()
 
     for g in range(GROUPS):
         span = slice(g * STATE, (g + 1) * STATE)
@@ -241,14 +285,22 @@
             sum_copy((place + distance) % RING, place, j).start()
         sum_in[place, j] = sum_out[place, j]
 
-    @pl.when(row == 0)
+    @pl.when(row < 2)
     def _():
         state_in[...] = jnp.zeros_like(state_in)
 
+    @pl.when(jnp.logical_not(second))
+    def _():
+        front_in[...] = jnp.zeros_like(front_in)
+        fade_in[...] = jnp.zeros_like(fade_in)
+
+    def spread_row(ref, j):
+        return jnp.concatenate(
+            [jnp.exp2(ref[pl.ds(j * PAIRS + p, 1), :]) for p in range(PAIRS)], axis=1
+        )
+
     def factor(source, j):
-        return jnp.concatenate(
-            [jnp.exp2(end_in[source, pl.ds(j * PAIRS + p, 1), :]) for p in range(PAIRS)], axis=1
-        )
+        return spread_row(end_in.at[source], j)
 
     def relay(j):
         for distance in range(1, RING):
@@ -261,26 +313,40 @@
             whole = whole * one
             summed = summed * one + sum_in[block, j].astype(F32)
 
-        @pl.when(row > 0)
-        def _():
-            state_copy(j).wait_recv()
-
-        @pl.when(row < rows - 1)
-        def _():
-            entering = state_in[j].astype(F32)
-            state_out[j] = (entering * whole + summed).astype(BF16)
-            state_copy(j).start()
+        @pl.when(jnp.logical_not(second))
+        def _():
+            front_out[j] = summed.astype(BF16)
+            front_copy(j).start()
+
+        @pl.when(second)
+        def _():
+            front_copy(j).wait_recv()
+
+            @pl.when(row > 1)
+            def _():
+                state_copy(j, 1).wait_recv()
+
+        @pl.when(passes_on)
+        def _():
+            state_out[j] = (entering(j) * whole + summed).astype(BF16)
+            state_copy(j, 2).start()
+            state_copy(j, 1).start()
+
+    def entering(j):
+        return state_in[j].astype(F32) * spread_row(fade_in, j) + front_in[j].astype(F32)
 
     def hand_back(j):
-        state = state_in[j].astype(F32)
-        back_out[0, j] = state_in[j]
+        @pl.when(jnp.logical_not(second) & (row > 0))
+        def _():
+            state_copy(j, 1).wait_recv()
+
+        state = entering(j)
+        back_out[0, j] = state.astype(BF16)
         for block in range(1, RING):
             state = state * factor(block - 1, j) + sum_in[block - 1, j].astype(F32)
             back_out[block, j] = state.astype(BF16)
-        for distance in range(1, RING):
-            to = (place + distance) % RING
-            back_copy(to, place, j).start()
-        back_in[place, j] = back_out[place, j]
+        for distance in (2, 1, 3, 0):
+            back_copy((place + distance) % RING, place, j).start()
 
     def within(j):
         cols = columns(cum_cols, j)
@@ -290,11 +356,9 @@
             for p in range(PAIRS):
                 at = pair_lanes(chunk, p)
                 weights = []
-                spread = []
                 for k in range(2):
                     lane_at = q * (HEADS // RING) + 2 * p + k
                     decay = jnp.broadcast_to(cols[:, lane_at : lane_at + 1], (SPAN, SPAN))
-                    spread.append(decay)
                     row_at = pl.ds(chunk * CHUNK_HEADS + 2 * p + k, 1)
                     weight = score * jnp.exp2(decay - shift_rows[row_at, :])
                     weights.append(jnp.where(causal, weight, 0.0).astype(BF16))
@@ -308,95 +372,104 @@
                 )
                 head = chunk * CHUNK_HEADS + 2 * p
                 skip = jnp.where(low[:1], skip_ref[0, head], skip_ref[0, head + 1])
-                total[:, at] = x_ref[:, at].astype(F32) + inner + skip * both.astype(F32)
-                grown[:, at] = jnp.exp2(jnp.where(low, spread[0], spread[1]))
+                part = x_ref[:, at].astype(F32) + inner + skip * both.astype(F32)
+                part_out[chunk, :, p * 128 : (p + 1) * 128] = part.astype(BF16)
+        for q in range(RING):
+            part_copy(q * CHUNKS + j).start()
+
+    def spread_decay(j):
+        cols = columns(cum_in, j)
+        for q in range(RING):
+            chunk = q * CHUNKS + j
+            for p in range(PAIRS):
+                lane_at = q * (HEADS // RING) + 2 * p
+                spread = jnp.where(
+                    low, cols[:, lane_at : lane_at + 1], cols[:, lane_at + 1 : lane_at + 2]
+                )
+                grown[:, pair_lanes(chunk, p)] = jnp.exp2(spread)
 
     def finish(j):
-        for distance in range(1, RING):
-            source = (place + distance) % RING
-            back_copy(source, source, j).wait_recv()
+        for q in range(RING):
+            back_copy(place, q, j).wait_recv()
+            part_copy(q * CHUNKS + j).wait_recv()
         for q in range(RING):
             chunk = q * CHUNKS + j
             lanes = lanes_of(chunk)
             group = pl.ds(pl.multiple_of((chunk // GROUP_CHUNKS) * STATE, STATE), STATE)
-            carried = jnp.dot(read_ref[:, group], back_in[q, j], preferred_element_type=F32)
-            last_out[chunk] = (total[:, lanes] + grown[:, lanes] * carried).astype(BF16)
-        for q in range(RING):
-            last_copy(q * CHUNKS + j).start()
-
-    early = jnp.where(row == 0, 3, 0)
-    begun = CHUNKS - early
-
-    def first_steps(i, carry):
-        produce(i)
-
-        @pl.when(i == 0)
+            carried = jnp.dot(read_in[:, group], back_in[q, j], preferred_element_type=F32)
+            out_ref[:, lanes] = (part_in[chunk].astype(F32) + grown[:, lanes] * carried).astype(
+                BF16
+            )
+
+    relay_lag = jnp.where(second, jnp.minimum(ODD + row, CHUNKS), EVEN)
+    back_lag = jnp.where(second, jnp.maximum(relay_lag + LAG - row, CHUNKS), EVEN + LAG)
+    finish_lag = back_lag + LATER
+
+    def only(j, step):
+        @pl.when((j >= 0) & (j < CHUNKS))
+        def _():
+            step(j)
+
+    def pipeline(i, carry):
+        only(i, produce)
+
+        @pl.when(i == 2)
         def _():
             for distance in range(1, RING):
                 source = (place + distance) % RING
                 end_copy(source, place).wait_send()
                 end_copy(source, source).wait_recv()
-
-        @pl.when(i >= begun)
-        def _():
-            relay(i - begun)
-
+            for copy in map_copies(0, 1):
+                copy.wait()
+
+            @pl.when(jnp.logical_not(second))
+            def _():
+                fade_out[...] = (end_in[0] + end_in[1]) + (end_in[2] + end_in[3])
+                fade_copy().start()
+
+            @pl.when(second)
+            def _():
+                fade_copy().wait_recv()
+
+        only(i - relay_lag, relay)
+        only(i - back_lag, hand_back)
+        only(i, within)
+        only(i - 2, spread_decay)
+        only(i - finish_lag, finish)
         return carry
 
-    lax.fori_loop(0, CHUNKS, first_steps, 0)
-
-    def only_within(i, carry):
-        within(i)
-        return carry
-
-    ahead = jnp.clip(5 * row - 4, 0, CHUNKS)
-    lax.fori_loop(0, ahead, only_within, 0)
-    lag = jnp.maximum(rows - 1 - row, 0)
-
-    def last_steps(i, carry):
-        @pl.when(i < CHUNKS)
-        def _():
-            relay(i)
-
-        j = i - lag
-
-        @pl.when((j >= 0) & (j < CHUNKS))
-        def _():
-            hand_back(j)
-
-        piece = ahead + i - early
-
-        @pl.when(piece < CHUNKS)
-        def _():
-            within(piece)
-
-        @pl.when(j >= 1)
-        def _():
-            finish(j - 1)
-
-        return carry
-
-    lax.fori_loop(early, lag + CHUNKS + 1, last_steps, 0)
+    lax.fori_loop(0, CHUNKS + finish_lag, pipeline, 0)
 
     def settle(j, carry):
         for distance in range(1, RING):
             to = (place + distance) % RING
             sum_copy(to, place, j).wait_send()
+
+        for to in range(RING):
             back_copy(to, place, j).wait_send()
 
         @pl.when(ctx < blocks - 1)
         def _():
             halo_copy(j).wait_send()
 
-        @pl.when(row < rows - 1)
-        def _():
-            state_copy(j).wait_send()
-
-        for q in range(RING):
-            last_copy(q * CHUNKS + j).wait()
+        @pl.when(passes_on)
+        def _():
+            state_copy(j, 2).wait_send()
+            state_copy(j, 1).wait_send()
+
+        @pl.when(jnp.logical_not(second))
+        def _():
+            front_copy(j).wait_send()
+
+        for q in range(RING):
+            part_copy(q * CHUNKS + j).wait_send()
         return carry
 
     lax.fori_loop(0, CHUNKS, settle, 0)
+
+    @pl.when(jnp.logical_not(second))
+    def _():
+        fade_copy().wait_send()
 
 
 def shards(
@@ -424,7 +497,6 @@
             pltpu.VMEM((RING * PAIRS, SPAN + 8, 128), F32),
             pltpu.VMEM((SPAN, WIDTH), BF16),
             pltpu.VMEM((SPAN, WIDTH), F32),
-            pltpu.VMEM((SPAN, WIDTH), F32),
             pltpu.VMEM((GROUPS, SPAN, SPAN), F32),
             pltpu.VMEM((GROUPS, STATE, SPAN), BF16),
             pltpu.VMEM((HEADS, SPAN), F32),
@@ -439,16 +511,26 @@
             pltpu.VMEM(half, BF16),
             pltpu.VMEM(half[1:], BF16),
             pltpu.VMEM(half[1:], BF16),
+            pltpu.VMEM(half[1:], BF16),
+            pltpu.VMEM(half[1:], BF16),
+            pltpu.VMEM((CHUNKS * PAIRS, 128), F32),
+            pltpu.VMEM((CHUNKS * PAIRS, 128), F32),
             pltpu.VMEM(half, BF16),
             pltpu.VMEM(half, BF16),
             pltpu.VMEM((chunks, SPAN, LANES), BF16),
+            pltpu.VMEM((chunks, SPAN, LANES), BF16),
+            pltpu.VMEM((SPAN, GROUPS * STATE), BF16),
+            pltpu.VMEM((SPAN, HEADS), F32),
             dma((8,)),
             dma((2, CHUNKS)),
             dma((2, RING)),
             dma((2, RING, CHUNKS)),
+            dma((3, CHUNKS)),
             dma((2, CHUNKS)),
+            dma((2,)),
             dma((2, RING, CHUNKS)),
             dma((2, chunks)),
+            dma((2, 2)),
         ],
         compiler_params=pltpu.CompilerParams(
             collective_id=0, has_side_effects=True, vmem_limit_bytes=48 << 20

time: 67.2 us -> 62.4 us (0.929)
  the two profiles are of different devices: /device:TPU:225 before, /device:TPU:96 now
where the time goes in v3:
time: 62.4 us; the launch traced here: 62.3 us
  Pallas kernels  60.4 us (97%)
  local copies, waits for them, and re-layouts  1.98 us (3%)
    pallas_call x1, Pallas kernels, shards(): pl.pallas_call(mixing_kernel, out_shape=jax.ShapeDtypeStruct((SPAN, WIDTH...  60.4 us
    unnamed x3, local copies, waits for them, and re-layouts  1.98 us

profile of v3, /device:TPU:96, one launch (start us, length us, event | category | flops | bytes accessed | tf_op | source)
XLA Modules:
  0.0 62.3 jit_solution(3870000320306934638)
XLA Ops:
  0.0 0.0 copy-start
  0.0 0.7 %copy-done = f32[1,128]{1,0:T(1,128)S(1)} copy-done((f32[1,128]{1,0:T(1,128)S(1)}, f32[1,128]{1,0:T(1,128)}, u32[]{:S(2)}) %copy-start) | copy-done | bytes 536
  0.7 60.4 %shard_map.82 = bf16[128,8192]{1,0:T(8,128)(2,1)S(1)} custom-call(bf16[128,8192]{1,0:T(8,128)(2,1)} %bitcast.8, bf16[1,8192]{1,0:T(2,128)(2,1)} %gain_hbm.1, bf16[4,8192]{1,0:T(4,128)(2,1)} %bitcast.11, bf16[128,1024]{1,0:T(8,128)(2,1)} %bitcast.9, bf16[128,1024]{1,0:T(8,128)(2,1)} %bitcast.10, f32[128,128]{1,0:T(8,128)} %bitcast.12, f32[128,128]{1,0:T(8,128)} %bitcast.13, ...), custom_call_target="tpu_custom_call" | custom-call | tf_op jit(solution)/shard_map/pallas_call | solution.py:483
  61.0 1.3 %copy.10 = bf16[1,128,8192]{2,1,0:T(8,128)(2,1)} copy(bf16[1,128,8192]{2,1,0:T(8,128)(2,1)S(1)} %bitcast.7) | data formatting | bytes 4194304
Async XLA Ops:
  0.0 0.7 %copy-start = (f32[1,128]{1,0:T(1,128)S(1)}, f32[1,128]{1,0:T(1,128)}, u32[]{:S(2)}) copy-start(f32[1,128]{1,0:T(1,128)} %skip_ref.1) | copy-start | bytes 1540

commit v4 on v3

--- a/solution.py
+++ b/solution.py
@@ -28,9 +28,9 @@
 
 
 def mixing_kernel(
-    x_hbm, gain_hbm, taps_hbm, write_hbm, read_hbm, step_hbm, decay_hbm, skip_ref,
+    x_hbm, gain_hbm, taps_hbm, write_hbm, read_hbm, step_hbm, decay_hbm, skip_hbm,
     out_ref,
-    x_ref, gain_ref, taps_ref, write_ref, read_ref, step_ref, decay_ref,
+    x_ref, gain_ref, taps_ref, write_ref, read_ref, step_ref, decay_ref, skip_ref,
     scale_buf, padded, mixed, grown, scores, write_t, cum_rows, cum_cols, shift_rows, shift_cols,
     halo_out, halo_in, end_out, end_in, sum_out, sum_in, state_in, state_out,
     front_out, front_in, fade_out, fade_in,
@@ -55,6 +55,25 @@
 
     def next_layer(index):
         return {"section": after_section, "ctx": row * RING + index}
+
+    barrier = pltpu.get_barrier_semaphore()
+    for index in range(RING):
+        holder = {"section": before_section, "ctx": row * RING + index}
+        pl.semaphore_signal(barrier, 1, device_id=holder)
+    for distance in range(1, RING):
+        pl.semaphore_signal(barrier, 1, device_id=at_place((place + distance) % RING))
+
+    @pl.when(ctx > 0)
+    def _():
+        pl.semaphore_signal(barrier, 1, device_id=at_ctx(before_ctx))
+
+    @pl.when(row > 0)
+    def _():
+        pl.semaphore_signal(barrier, 1, device_id=at_ctx(ctx - RING))
+
+    @pl.when(second & (row > 1))
+    def _():
+        pl.semaphore_signal(barrier, 1, device_id=at_ctx(ctx - 2 * RING))
 
     late = SPAN - 16
     fetches = [
@@ -69,30 +88,12 @@
                 (taps_hbm, taps_ref),
                 (write_hbm, write_ref),
                 (read_hbm, read_ref),
+                (skip_hbm, skip_ref),
             ]
         )
     ]
     for fetch in fetches:
         fetch.start()
-
-    barrier = pltpu.get_barrier_semaphore()
-    for index in range(RING):
-        holder = {"section": before_section, "ctx": row * RING + index}
-        pl.semaphore_signal(barrier, 1, device_id=holder)
-    for distance in range(1, RING):
-        pl.semaphore_signal(barrier, 1, device_id=at_place((place + distance) % RING))
-
-    @pl.when(ctx > 0)
-    def _():
-        pl.semaphore_signal(barrier, 1, device_id=at_ctx(before_ctx))
-
-    @pl.when(row > 0)
-    def _():
-        pl.semaphore_signal(barrier, 1, device_id=at_ctx(ctx - RING))
-
-    @pl.when(second & (row > 1))
-    def _():
-        pl.semaphore_signal(barrier, 1, device_id=at_ctx(ctx - 2 * RING))
 
     def halo_copy(j):
         return pltpu.make_async_remote_copy(
@@ -250,6 +251,12 @@
     scale_buf[...] = scale
 
     def produce(j):
+        for q in range(RING):
+            for p in range(PAIRS):
+                at = pair_lanes(q * CHUNKS + j, p)
+                normed = (x_ref[:, at].astype(F32) * scale_buf[...]) * gain_ref[:, at].astype(F32)
+                padded[q * PAIRS + p, 8:, :] = normed.astype(BF16).astype(F32)
+
         @pl.when(ctx > 0)
         def _():
             halo_copy(j).wait_recv()
@@ -261,8 +268,6 @@
             for p in range(PAIRS):
                 at = pair_lanes(chunk, p)
                 buffer = padded.at[q * PAIRS + p]
-                normed = (x_ref[:, at].astype(F32) * scale_buf[...]) * gain_ref[:, at].astype(F32)
-                buffer[8:, :] = normed.astype(BF16).astype(F32)
                 buffer[8 - (CONV - 1) : 8, :] = halo_in[j, q, 4 * p : 4 * p + 3, :]
                 taps = taps_ref[:, at].astype(F32)
                 acc = taps[0:1, :] * buffer[8 - (CONV - 1) : 8 - (CONV - 1) + SPAN, :]
@@ -483,7 +488,7 @@
     handed = pl.pallas_call(
         mixing_kernel,
         out_shape=jax.ShapeDtypeStruct((SPAN, WIDTH), BF16),
-        in_specs=[hbm] * 7 + [pl.BlockSpec(memory_space=pltpu.SMEM)],
+        in_specs=[hbm] * 8,
         out_specs=pl.BlockSpec(memory_space=pltpu.VMEM),
         scratch_shapes=[
             pltpu.VMEM((SPAN, WIDTH), BF16),
@@ -493,6 +498,7 @@
             pltpu.VMEM((SPAN, GROUPS * STATE), BF16),
             pltpu.VMEM((HEADS, SPAN), F32),
             pltpu.VMEM((HEADS, SPAN), F32),
+            pltpu.SMEM((1, HEADS), F32),
             pltpu.VMEM((SPAN, 128), F32),
             pltpu.VMEM((RING * PAIRS, SPAN + 8, 128), F32),
             pltpu.VMEM((SPAN, WIDTH), BF16),
@@ -521,7 +527,7 @@
             pltpu.VMEM((chunks, SPAN, LANES), BF16),
             pltpu.VMEM((SPAN, GROUPS * STATE), BF16),
             pltpu.VMEM((SPAN, HEADS), F32),
-            dma((8,)),
+            dma((9,)),
             dma((2, CHUNKS)),
             dma((2, RING)),
             dma((2, RING, CHUNKS)),
@@ -546,9 +552,9 @@
                 state_read[0],
                 step_size[0],
                 log_decay[0],
+                skip_gain,
             )
-        ),
-        skip_gain,
+        )
     )
     return handed[None]
 

time: 62.4 us -> 61.1 us (0.979)
  Pallas kernels: 60.4 us -> 59.7 us
  local copies, waits for them, and re-layouts: 1.98 us -> 1.32 us
    unnamed x3 -> x1, local copies, waits for them, and re-layouts: 1.98 us -> 1.32 us
    pallas_call x1, Pallas kernels: 60.4 us -> 59.7 us  [shards(): pl.pallas_call(mixing_kernel, out_shape=jax.ShapeDtypeStruct((SPAN, WIDTH...]
where the time goes in v4:
time: 61.1 us; the launch traced here: 61 us
  Pallas kernels  59.7 us (98%)
  local copies, waits for them, and re-layouts  1.32 us (2%)
    pallas_call x1, Pallas kernels, shards(): pl.pallas_call(mixing_kernel, out_shape=jax.ShapeDtypeStruct((SPAN, WIDTH...  59.7 us
    unnamed x1, local copies, waits for them, and re-layouts  1.32 us

profile of v4, /device:TPU:96, one launch (start us, length us, event | category | flops | bytes accessed | tf_op | source)
XLA Modules:
  0.0 61.0 jit_solution(15659147261923624515)
XLA Ops:
  0.0 59.7 %shard_map.82 = bf16[128,8192]{1,0:T(8,128)(2,1)S(1)} custom-call(bf16[128,8192]{1,0:T(8,128)(2,1)} %bitcast.8, bf16[1,8192]{1,0:T(2,128)(2,1)} %gain_hbm.1, bf16[4,8192]{1,0:T(4,128)(2,1)} %bitcast.11, bf16[128,1024]{1,0:T(8,128)(2,1)} %bitcast.9, bf16[128,1024]{1,0:T(8,128)(2,1)} %bitcast.10, f32[128,128]{1,0:T(8,128)} %bitcast.12, f32[128,128]{1,0:T(8,128)} %bitcast.13, ...), custom_call_target="tpu_custom_call" | custom-call | tf_op jit(solution)/shard_map/pallas_call | solution.py:488
  59.7 1.3 %copy.10 = bf16[1,128,8192]{2,1,0:T(8,128)(2,1)} copy(bf16[1,128,8192]{2,1,0:T(8,128)(2,1)S(1)} %bitcast.7) | data formatting | bytes 4194304

commit v5 on v4

--- a/solution.py
+++ b/solution.py
@@ -22,6 +22,7 @@
 EVEN = 3
 ODD = 3
 LAG = 5
+END_ROWS = CHUNKS * PAIRS
 LOG2E = 1.4426950408889634
 F32 = jnp.float32
 BF16 = jnp.bfloat16
@@ -104,7 +105,7 @@
 
     def end_copy(to, slot):
         return pltpu.make_async_remote_copy(
-            src_ref=end_out.at[to], dst_ref=end_in.at[slot],
+            src_ref=end_out.at[to, pl.ds(0, END_ROWS)], dst_ref=end_in.at[slot, pl.ds(0, END_ROWS)],
             send_sem=end_sems.at[0, to], recv_sem=end_sems.at[1, slot], device_id=at_place(to),
         )
 
@@ -131,7 +132,7 @@
 
     def fade_copy():
         return pltpu.make_async_remote_copy(
-            src_ref=fade_out, dst_ref=fade_in, send_sem=fade_sems.at[0], recv_sem=fade_sems.at[1],
+            src_ref=fade_out, dst_ref=fade_in.at[pl.ds(0, END_ROWS)], send_sem=fade_sems.at[0], recv_sem=fade_sems.at[1],
             device_id=at_ctx((ctx + RING) % blocks),
         )
 
@@ -178,12 +179,18 @@
     fetches[0].wait()
     fetches[1].wait()
     tail_scale = square_sum(late, 16)
-    for chunk in range(RING * CHUNKS):
-        for p in range(PAIRS):
-            span = slice(chunk * LANES + p * 128, chunk * LANES + p * 128 + 128)
-            normed = (x_ref[late:SPAN, span].astype(F32) * tail_scale) * gain_ref[:, span].astype(F32)
-            normed = normed.astype(BF16).astype(F32)
-            halo_out[chunk % CHUNKS, chunk // CHUNKS, 4 * p : 4 * p + 3, :] = normed[13:16, :]
+    for j in range(CHUNKS):
+        for half in range(2):
+            pieces = []
+            for part in range(2 * PAIRS):
+                q, p = 2 * half + part // PAIRS, part % PAIRS
+                first = (q * CHUNKS + j) * LANES + p * 128
+                span = slice(first, first + 128)
+                normed = (x_ref[late:SPAN, span].astype(F32) * tail_scale) * gain_ref[
+                    :, span
+                ].astype(F32)
+                pieces.append(normed[12:16, :])
+            halo_out[j, half] = jnp.concatenate(pieces, axis=0).astype(BF16)
 
     pl.semaphore_wait(
         barrier,
@@ -216,16 +223,17 @@
         jnp.broadcast_to(cum_rows[pl.ds(first, HEADS // 2, stride=2), :][:, SPAN - 1 :], (HEADS // 2, 128))
         for first in range(2)
     )
-    end_out[...] = jnp.where(low[: HEADS // 2], even, odd).reshape(RING, CHUNKS * PAIRS, 128)
+    ends = jnp.where(low[: HEADS // 2], even, odd)
+    end_out[:, pl.ds(0, END_ROWS), :] = ends.reshape(RING, END_ROWS, 128)
     for distance in range(1, RING):
         to = (place + distance) % RING
         end_copy(to, place).start()
-    end_in[place] = end_out[place]
+    end_in[place, pl.ds(0, END_ROWS), :] = end_out[place, pl.ds(0, END_ROWS), :]
     cum_cols[...] = cumul.T
     map_copies(0)[0].start()
     fetches[3].wait()
     shift = cumul - jnp.log2(step_ref[...])
-    shift_rows[...] = shift
+    shift_rows[pl.ds(0, HEADS), :] = shift
     shift_cols[...] = shift.T
 
     fetches[4].wait()
@@ -261,6 +269,7 @@
         def _():
             halo_copy(j).wait_recv()
 
+        before = [halo_in[j, half].astype(F32) for half in range(2)]
         cols = columns(shift_cols, j)
         for q in range(RING):
             chunk = q * CHUNKS + j
@@ -268,7 +277,8 @@
             for p in range(PAIRS):
                 at = pair_lanes(chunk, p)
                 buffer = padded.at[q * PAIRS + p]
-                buffer[8 - (CONV - 1) : 8, :] = halo_in[j, q, 4 * p : 4 * p + 3, :]
+                first = 4 * (q % 2 * PAIRS + p)
+                buffer[4:8, :] = before[q // 2][first : first + 4, :]
                 taps = taps_ref[:, at].astype(F32)
                 acc = taps[0:1, :] * buffer[8 - (CONV - 1) : 8 - (CONV - 1) + SPAN, :]
                 for k in range(1, CONV):
@@ -394,17 +404,41 @@
                 grown[:, pair_lanes(chunk, p)] = jnp.exp2(spread)
 
     def finish(j):
-        for q in range(RING):
-            back_copy(place, q, j).wait_recv()
-            part_copy(q * CHUNKS + j).wait_recv()
-        for q in range(RING):
+        for distance in (0, 1, 3, 2):
+            q = (place + distance) % RING
             chunk = q * CHUNKS + j
             lanes = lanes_of(chunk)
             group = pl.ds(pl.multiple_of((chunk // GROUP_CHUNKS) * STATE, STATE), STATE)
+            part_copy(chunk).wait_recv()
+            back_copy(place, q, j).wait_recv()
             carried = jnp.dot(read_in[:, group], back_in[q, j], preferred_element_type=F32)
             out_ref[:, lanes] = (part_in[chunk].astype(F32) + grown[:, lanes] * carried).astype(
                 BF16
             )
+
+    def settle(j):
+        for distance in range(1, RING):
+            to = (place + distance) % RING
+            sum_copy(to, place, j).wait_send()
+
+        for to in range(RING):
+            back_copy(to, place, j).wait_send()
+
+        @pl.when(ctx < blocks - 1)
+        def _():
+            halo_copy(j).wait_send()
+
+        @pl.when(passes_on)
+        def _():
+            state_copy(j, 2).wait_send()
+            state_copy(j, 1).wait_send()
+
+        @pl.when(jnp.logical_not(second))
+        def _():
+            front_copy(j).wait_send()
+
+        for q in range(RING):
+            part_copy(q * CHUNKS + j).wait_send()
 
     relay_lag = jnp.where(second, jnp.minimum(ODD + row, CHUNKS), EVEN)
     back_lag = jnp.where(second, jnp.maximum(relay_lag + LAG - row, CHUNKS), EVEN + LAG)
@@ -429,7 +463,8 @@
 
             @pl.when(jnp.logical_not(second))
             def _():
-                fade_out[...] = (end_in[0] + end_in[1]) + (end_in[2] + end_in[3])
+                ends = [end_in[block, pl.ds(0, END_ROWS), :] for block in range(RING)]
+                fade_out[...] = (ends[0] + ends[1]) + (ends[2] + ends[3])
                 fade_copy().start()
 
             @pl.when(second)
@@ -440,37 +475,11 @@
         only(i - back_lag, hand_back)
         only(i, within)
         only(i - 2, spread_decay)
+        only(i - finish_lag, settle)
         only(i - finish_lag, finish)
         return carry
 
     lax.fori_loop(0, CHUNKS + finish_lag, pipeline, 0)
-
-    def settle(j, carry):
-        for distance in range(1, RING):
-            to = (place + distance) % RING
-            sum_copy(to, place, j).wait_send()
-
-        for to in range(RING):
-            back_copy(to, place, j).wait_send()
-
-        @pl.when(ctx < blocks - 1)
-        def _():
-            halo_copy(j).wait_send()
-
-        @pl.when(passes_on)
-        def _():
-            state_copy(j, 2).wait_send()
-            state_copy(j, 1).wait_send()
-
-        @pl.when(jnp.logical_not(second))
-        def _():
-            front_copy(j).wait_send()
-
-        for q in range(RING):
-            part_copy(q * CHUNKS + j).wait_send()
-        return carry
-
-    lax.fori_loop(0, CHUNKS, settle, 0)
 
     @pl.when(jnp.logical_not(second))
     def _():
@@ -484,7 +493,7 @@
     dma = pltpu.SemaphoreType.DMA
     chunks = WIDTH // LANES
     half = (RING, CHUNKS, STATE, LANES)
-    halo = (CHUNKS, RING, 8, 128)
+    halo = (CHUNKS, 2, 16, 128)
     handed = pl.pallas_call(
         mixing_kernel,
         out_shape=jax.ShapeDtypeStruct((SPAN, WIDTH), BF16),
@@ -507,20 +516,20 @@
             pltpu.VMEM((GROUPS, STATE, SPAN), BF16),
             pltpu.VMEM((HEADS, SPAN), F32),
             pltpu.VMEM((SPAN, HEADS), F32),
-            pltpu.VMEM((HEADS, SPAN), F32),
+            pltpu.VMEM((HEADS + 8, SPAN), F32),
             pltpu.VMEM((SPAN, HEADS), F32),
-            pltpu.VMEM(halo, F32),
-            pltpu.VMEM(halo, F32),
-            pltpu.VMEM((RING, CHUNKS * PAIRS, 128), F32),
-            pltpu.VMEM((RING, CHUNKS * PAIRS, 128), F32),
+            pltpu.VMEM(halo, BF16),
+            pltpu.VMEM(halo, BF16),
+            pltpu.VMEM((RING, END_ROWS + 8, 128), F32),
+            pltpu.VMEM((RING, END_ROWS + 8, 128), F32),
             pltpu.VMEM(half, BF16),
             pltpu.VMEM(half, BF16),
             pltpu.VMEM(half[1:], BF16),
             pltpu.VMEM(half[1:], BF16),
             pltpu.VMEM(half[1:], BF16),
             pltpu.VMEM(half[1:], BF16),
-            pltpu.VMEM((CHUNKS * PAIRS, 128), F32),
-            pltpu.VMEM((CHUNKS * PAIRS, 128), F32),
+            pltpu.VMEM((END_ROWS, 128), F32),
+            pltpu.VMEM((END_ROWS + 8, 128), F32),
             pltpu.VMEM(half, BF16),
             pltpu.VMEM(half, BF16),
             pltpu.VMEM((chunks, SPAN, LANES), BF16),

time: 61.1 us -> 61 us (level)
  no operation moved by 1% of the time
where the time goes in v5:
time: 61 us; the launch traced here: 60.9 us
  Pallas kernels  59.6 us (98%)
  local copies, waits for them, and re-layouts  1.32 us (2%)
    pallas_call x1, Pallas kernels, shards(): pl.pallas_call(mixing_kernel, out_shape=jax.ShapeDtypeStruct((SPAN, WIDTH...  59.6 us
    unnamed x1, local copies, waits for them, and re-layouts  1.32 us

profile of v5, /device:TPU:96, one launch (start us, length us, event | category | flops | bytes accessed | tf_op | source)
XLA Modules:
  0.0 60.9 jit_solution(13207781252895362212)
XLA Ops:
  0.0 59.6 %shard_map.82 = bf16[128,8192]{1,0:T(8,128)(2,1)S(1)} custom-call(bf16[128,8192]{1,0:T(8,128)(2,1)} %bitcast.8, bf16[1,8192]{1,0:T(2,128)(2,1)} %gain_hbm.1, bf16[4,8192]{1,0:T(4,128)(2,1)} %bitcast.11, bf16[128,1024]{1,0:T(8,128)(2,1)} %bitcast.9, bf16[128,1024]{1,0:T(8,128)(2,1)} %bitcast.10, f32[128,128]{1,0:T(8,128)} %bitcast.12, f32[128,128]{1,0:T(8,128)} %bitcast.13, ...), custom_call_target="tpu_custom_call" | custom-call | tf_op jit(solution)/shard_map/pallas_call | solution.py:497
  59.6 1.3 %copy.10 = bf16[1,128,8192]{2,1,0:T(8,128)(2,1)} copy(bf16[1,128,8192]{2,1,0:T(8,128)(2,1)S(1)} %bitcast.7) | data formatting | bytes 4194304

commit v6 on v5

--- a/solution.py
+++ b/solution.py
@@ -34,9 +34,9 @@
     x_ref, gain_ref, taps_ref, write_ref, read_ref, step_ref, decay_ref, skip_ref,
     scale_buf, padded, mixed, grown, scores, write_t, cum_rows, cum_cols, shift_rows, shift_cols,
     halo_out, halo_in, end_out, end_in, sum_out, sum_in, state_in, state_out,
-    front_out, front_in, fade_out, fade_in,
+    front_out, front_in, fade_out, fade_in, head_out, head_in,
     back_out, back_in, part_out, part_in, read_in, cum_in,
-    fetch_sems, halo_sems, end_sems, sum_sems, state_sems, front_sems, fade_sems, back_sems, part_sems, map_sems,
+    fetch_sems, halo_sems, end_sems, head_sems, sum_sems, state_sems, front_sems, fade_sems, back_sems, part_sems, map_sems,
 ):
     sections, blocks = lax.axis_size("section"), lax.axis_size("ctx")
     rows = blocks // RING
@@ -116,6 +116,12 @@
             device_id=at_place(to),
         )
 
+    def head_copy(to, slot):
+        return pltpu.make_async_remote_copy(
+            src_ref=head_out.at[to], dst_ref=head_in.at[slot],
+            send_sem=head_sems.at[0, to], recv_sem=head_sems.at[1, slot], device_id=at_place(to),
+        )
+
     def state_copy(j, hops):
         return pltpu.make_async_remote_copy(
             src_ref=state_out.at[j], dst_ref=state_in.at[j],
@@ -191,22 +197,6 @@
                 ].astype(F32)
                 pieces.append(normed[12:16, :])
             halo_out[j, half] = jnp.concatenate(pieces, axis=0).astype(BF16)
-
-    pl.semaphore_wait(
-        barrier,
-        2 * RING - 1
-        + jnp.where(ctx < blocks - 1, 1, 0)
-        + jnp.where(second, jnp.where(row < rows - 1, 2, 0), 1),
-    )
-
-    @pl.when(ctx < blocks - 1)
-    def _():
-        for j in range(CHUNKS):
-            halo_copy(j).start()
-
-    @pl.when(ctx == 0)
-    def _():
-        halo_in[...] = jnp.zeros_like(halo_in)
 
     token = lax.broadcasted_iota(jnp.int32, (SPAN, SPAN), 0)
     lane = lax.broadcasted_iota(jnp.int32, (SPAN, SPAN), 1)
@@ -225,12 +215,8 @@
     )
     ends = jnp.where(low[: HEADS // 2], even, odd)
     end_out[:, pl.ds(0, END_ROWS), :] = ends.reshape(RING, END_ROWS, 128)
-    for distance in range(1, RING):
-        to = (place + distance) % RING
-        end_copy(to, place).start()
     end_in[place, pl.ds(0, END_ROWS), :] = end_out[place, pl.ds(0, END_ROWS), :]
     cum_cols[...] = cumul.T
-    map_copies(0)[0].start()
     fetches[3].wait()
     shift = cumul - jnp.log2(step_ref[...])
     shift_rows[pl.ds(0, HEADS), :] = shift
@@ -240,14 +226,9 @@
     scale = square_sum(0, SPAN)
     for fetch in fetches[5:]:
         fetch.wait()
-    map_copies(1)[0].start()
 
     for g in range(GROUPS):
-        span = slice(g * STATE, (g + 1) * STATE)
-        writes = write_ref[:, span]
-        scores[g] = lax.dot_general(
-            read_ref[:, span], writes, (((1,), (1,)), ((), ())), preferred_element_type=F32
-        )
+        writes = write_ref[:, g * STATE : (g + 1) * STATE]
         write_t[g] = writes.astype(F32).T.astype(BF16)
 
     def columns(ref, j):
@@ -258,47 +239,124 @@
 
     scale_buf[...] = scale
 
-    def produce(j):
+    def norm_chunk(j):
         for q in range(RING):
             for p in range(PAIRS):
                 at = pair_lanes(q * CHUNKS + j, p)
                 normed = (x_ref[:, at].astype(F32) * scale_buf[...]) * gain_ref[:, at].astype(F32)
                 padded[q * PAIRS + p, 8:, :] = normed.astype(BF16).astype(F32)
 
+    def take_halo(j):
         @pl.when(ctx > 0)
         def _():
             halo_copy(j).wait_recv()
 
         before = [halo_in[j, half].astype(F32) for half in range(2)]
+        for q in range(RING):
+            for p in range(PAIRS):
+                first = 4 * (q % 2 * PAIRS + p)
+                padded[q * PAIRS + p, 4:8, :] = before[q // 2][first : first + 4, :]
+
+    def mix(j, q, p, count, cols):
+        at = pair_lanes(q * CHUNKS + j, p)
+        buffer = padded.at[q * PAIRS + p]
+        taps = taps_ref[:, at].astype(F32)
+        acc = taps[0:1, :] * buffer[8 - (CONV - 1) : 8 - (CONV - 1) + count, :]
+        for k in range(1, CONV):
+            first = 8 - (CONV - 1) + k
+            acc = acc + taps[k : k + 1, :] * buffer[first : first + count, :]
+        acc = acc * (0.5 + 0.5 * jnp.tanh(0.5 * acc))
+        value = acc.astype(BF16)
+        mixed[pl.ds(0, count), at] = value
+        head = q * (HEADS // RING) + 2 * p
+        spread = jnp.where(
+            low[:count], cols[:count, head : head + 1], cols[:count, head + 1 : head + 2]
+        )
+        end = end_out[q, pl.ds(j * PAIRS + p, 1), :]
+        return value.astype(F32) * jnp.exp2(end - spread)
+
+    def send_sums(j):
+        for distance in (2, 1, 3):
+            sum_copy((place + distance) % RING, place, j).start()
+        sum_in[place, j] = sum_out[place, j]
+
+    def summarize(j, kept):
         cols = columns(shift_cols, j)
         for q in range(RING):
-            chunk = q * CHUNKS + j
-            parts = []
-            for p in range(PAIRS):
-                at = pair_lanes(chunk, p)
-                buffer = padded.at[q * PAIRS + p]
-                first = 4 * (q % 2 * PAIRS + p)
-                buffer[4:8, :] = before[q // 2][first : first + 4, :]
-                taps = taps_ref[:, at].astype(F32)
-                acc = taps[0:1, :] * buffer[8 - (CONV - 1) : 8 - (CONV - 1) + SPAN, :]
-                for k in range(1, CONV):
-                    first = 8 - (CONV - 1) + k
-                    acc = acc + taps[k : k + 1, :] * buffer[first : first + SPAN, :]
-                acc = acc * (0.5 + 0.5 * jnp.tanh(0.5 * acc))
-                value = acc.astype(BF16)
-                mixed[:, at] = value
-                head = q * (HEADS // RING) + 2 * p
-                spread = jnp.where(low, cols[:, head : head + 1], cols[:, head + 1 : head + 2])
-                end = end_out[q, pl.ds(j * PAIRS + p, 1), :]
-                parts.append((value.astype(F32) * jnp.exp2(end - spread)).astype(BF16))
+            parts = [kept(mix(j, q, p, SPAN, cols)).astype(BF16) for p in range(PAIRS)]
             sum_out[q, j] = jnp.dot(
-                write_t[chunk // GROUP_CHUNKS],
+                write_t[(q * CHUNKS + j) // GROUP_CHUNKS],
                 jnp.concatenate(parts, axis=1),
                 preferred_element_type=F32,
             ).astype(BF16)
-        for distance in (2, 1, 3):
-            sum_copy((place + distance) % RING, place, j).start()
-        sum_in[place, j] = sum_out[place, j]
+        send_sums(j)
+
+    def produce(j):
+        norm_chunk(j)
+        take_halo(j)
+        summarize(j, lambda scaled: scaled)
+
+    def produce_first():
+        for q in range(RING * PAIRS):
+            padded[q, 0:8, :] = jnp.zeros((8, 128), F32)
+        norm_chunk(0)
+        summarize(0, lambda scaled: jnp.where(token >= CONV - 1, scaled, 0.0))
+
+    def complete_first():
+        take_halo(0)
+        cols = columns(shift_cols, 0)
+        for q in range(RING):
+            parts = [
+                jnp.where(token[:16] < CONV - 1, mix(0, q, p, 16, cols), 0.0).astype(BF16)
+                for p in range(PAIRS)
+            ]
+            group = q * CHUNKS // GROUP_CHUNKS * STATE
+            parts.append(write_ref[0:16, group : group + STATE])
+            head_out[q] = jnp.concatenate(parts, axis=1)
+        for distance in range(1, RING):
+            head_copy((place + distance) % RING, place).start()
+        head_in[place] = head_out[place]
+
+    def add_first():
+        for distance in range(1, RING):
+            source = (place + distance) % RING
+            head_copy(source, source).wait_recv()
+            sum_copy(source, source, 0).wait_recv()
+        for source in range(RING):
+            maps = head_in[source, :, LANES:].astype(F32).T.astype(BF16)
+            added = jnp.dot(maps, head_in[source, :, :LANES], preferred_element_type=F32)
+            sum_in[source, 0] = (sum_in[source, 0].astype(F32) + added).astype(BF16)
+
+    pl.semaphore_wait(
+        barrier,
+        2 * RING - 1
+        + jnp.where(ctx < blocks - 1, 1, 0)
+        + jnp.where(second, jnp.where(row < rows - 1, 2, 0), 1),
+    )
+
+    @pl.when(ctx < blocks - 1)
+    def _():
+        for j in range(CHUNKS):
+            halo_copy(j).start()
+
+    @pl.when(ctx == 0)
+    def _():
+        halo_in[...] = jnp.zeros_like(halo_in)
+
+    for distance in range(1, RING):
+        to = (place + distance) % RING
+        end_copy(to, place).start()
+    for copy in map_copies(0, 1):
+        copy.start()
+
+    produce_first()
+    for g in range(GROUPS):
+        span = slice(g * STATE, (g + 1) * STATE)
+        scores[g] = lax.dot_general(
+            read_ref[:, span], write_ref[:, span], (((1,), (1,)), ((), ())),
+            preferred_element_type=F32,
+        )
+    complete_first()
 
     @pl.when(row < 2)
     def _():
@@ -318,9 +376,16 @@
         return spread_row(end_in.at[source], j)
 
     def relay(j):
-        for distance in range(1, RING):
-            source = (place + distance) % RING
-            sum_copy(source, source, j).wait_recv()
+        @pl.when(j == 0)
+        def _():
+            add_first()
+
+        @pl.when(j > 0)
+        def _():
+            for distance in range(1, RING):
+                source = (place + distance) % RING
+                sum_copy(source, source, j).wait_recv()
+
         whole = factor(0, j)
         summed = sum_in[0, j].astype(F32)
         for block in range(1, RING):
@@ -450,7 +515,9 @@
             step(j)
 
     def pipeline(i, carry):
-        only(i, produce)
+        @pl.when((i > 0) & (i < CHUNKS))
+        def _():
+            produce(i)
 
         @pl.when(i == 2)
         def _():
@@ -480,6 +547,9 @@
         return carry
 
     lax.fori_loop(0, CHUNKS + finish_lag, pipeline, 0)
+
+    for distance in range(1, RING):
+        head_copy((place + distance) % RING, place).wait_send()
 
     @pl.when(jnp.logical_not(second))
     def _():
@@ -530,6 +600,8 @@
             pltpu.VMEM(half[1:], BF16),
             pltpu.VMEM((END_ROWS, 128), F32),
             pltpu.VMEM((END_ROWS + 8, 128), F32),
+            pltpu.VMEM((RING, 16, LANES + STATE), BF16),
+            pltpu.VMEM((RING, 16, LANES + STATE), BF16),
             pltpu.VMEM(half, BF16),
             pltpu.VMEM(half, BF16),
             pltpu.VMEM((chunks, SPAN, LANES), BF16),
@@ -538,6 +610,7 @@
             pltpu.VMEM((SPAN, HEADS), F32),
             dma((9,)),
             dma((2, CHUNKS)),
+            dma((2, RING)),
             dma((2, RING)),
             dma((2, RING, CHUNKS)),
             dma((3, CHUNKS)),

time: 61 us -> 60.7 us (level)
  no operation moved by 1% of the time
where the time goes in v6:
time: 60.7 us; the launch traced here: 60.6 us
  Pallas kernels  59.3 us (98%)
  local copies, waits for them, and re-layouts  1.32 us (2%)
    pallas_call x1, Pallas kernels, shards(): pl.pallas_call(mixing_kernel, out_shape=jax.ShapeDtypeStruct((SPAN, WIDTH...  59.3 us
    unnamed x1, local copies, waits for them, and re-layouts  1.32 us

profile of v6, /device:TPU:96, one launch (start us, length us, event | category | flops | bytes accessed | tf_op | source)
XLA Modules:
  0.0 60.6 jit_solution(1532515838719660937)
XLA Ops:
  0.0 59.3 %shard_map.82 = bf16[128,8192]{1,0:T(8,128)(2,1)S(1)} custom-call(bf16[128,8192]{1,0:T(8,128)(2,1)} %bitcast.8, bf16[1,8192]{1,0:T(2,128)(2,1)} %gain_hbm.1, bf16[4,8192]{1,0:T(4,128)(2,1)} %bitcast.11, bf16[128,1024]{1,0:T(8,128)(2,1)} %bitcast.9, bf16[128,1024]{1,0:T(8,128)(2,1)} %bitcast.10, f32[128,128]{1,0:T(8,128)} %bitcast.12, f32[128,128]{1,0:T(8,128)} %bitcast.13, ...), custom_call_target="tpu_custom_call" | custom-call | tf_op jit(solution)/shard_map/pallas_call | solution.py:567
  59.3 1.3 %copy.10 = bf16[1,128,8192]{2,1,0:T(8,128)(2,1)} copy(bf16[1,128,8192]{2,1,0:T(8,128)(2,1)S(1)} %bitcast.7) | data formatting | bytes 4194304

commit v7 on v6

--- a/solution.py
+++ b/solution.py
@@ -21,7 +21,7 @@
 LATER = 3
 EVEN = 3
 ODD = 3
-LAG = 5
+LAG = 4
 END_ROWS = CHUNKS * PAIRS
 LOG2E = 1.4426950408889634
 F32 = jnp.float32

time: 60.7 us -> 60.7 us (level)
  no operation moved by 1% of the time
where the time goes in v7:
time: 60.7 us; the launch traced here: 60.6 us
  Pallas kernels  59.3 us (98%)
  local copies, waits for them, and re-layouts  1.32 us (2%)
    pallas_call x1, Pallas kernels, shards(): pl.pallas_call(mixing_kernel, out_shape=jax.ShapeDtypeStruct((SPAN, WIDTH...  59.3 us
    unnamed x1, local copies, waits for them, and re-layouts  1.32 us

profile of v7, /device:TPU:96, one launch (start us, length us, event | category | flops | bytes accessed | tf_op | source)
XLA Modules:
  0.0 60.6 jit_solution(16468631659118847687)
XLA Ops:
  0.0 59.3 %shard_map.82 = bf16[128,8192]{1,0:T(8,128)(2,1)S(1)} custom-call(bf16[128,8192]{1,0:T(8,128)(2,1)} %bitcast.8, bf16[1,8192]{1,0:T(2,128)(2,1)} %gain_hbm.1, bf16[4,8192]{1,0:T(4,128)(2,1)} %bitcast.11, bf16[128,1024]{1,0:T(8,128)(2,1)} %bitcast.9, bf16[128,1024]{1,0:T(8,128)(2,1)} %bitcast.10, f32[128,128]{1,0:T(8,128)} %bitcast.12, f32[128,128]{1,0:T(8,128)} %bitcast.13, ...), custom_call_target="tpu_custom_call" | custom-call | tf_op jit(solution)/shard_map/pallas_call | solution.py:567
  59.3 1.3 %copy.10 = bf16[1,128,8192]{2,1,0:T(8,128)(2,1)} copy(bf16[1,128,8192]{2,1,0:T(8,128)(2,1)S(1)} %bitcast.7) | data formatting | bytes 4194304
